TPU v7x, 128 devices: a whole 4x4x4 slice. The times are simulated.
128 devices in a mesh: row: 4 (over x_lo, core), col: 32 (over z, y, x_hi).
Axes of the slice: x: 4 (x_hi: 2, x_lo: 2; x = x_hi * 2 + x_lo), y: 4, z: 4, core: 2. Of those that a mesh axis runs over, the one named last changes fastest.
Arguments:
- matrix: float32 [16384, 16384], P('row', 'col'), as said below
- right_sides: float32 [16384, 256], P('row'), may hold values from -6 to 6
Outputs:
- factored: float32 [16384, 16384], P('row', 'col')
- solved: float32 [16384, 256], P('row')
Inputs may be any that keep to these rules, and one draw needn't show every extreme that they name: `matrix`: symmetric and positive definite in natural order.
All inputs are finite; a program needn't handle non-finite values.
Results may differ from a plain program's by a relative error of at most 0.0001.
Values sent between devices are 32-bit elements; how exact they have to be, the bound alone decides.
No kernel may reach another device: no remote copies, remote signals or barrier semaphores. Data moves between devices by JAX's collectives and lax.ppermute only.
A program may use at most 192 MiB of HBM per device.

v0:
```python
import jax
import jax.numpy as jnp
from jax import lax
from jax.sharding import PartitionSpec as P

NB = 512
PANELS = 2


def broadcast(block, axis, source):
    block = jnp.where(lax.axis_index(axis) == source, block, jnp.zeros_like(block))
    return lax.psum(block, axis)


def lower_panel(column, factor, row_ids, current, block_count):
    answer = jax.scipy.linalg.solve_triangular(factor, column.T, lower=True).T
    tiled = jnp.tile(factor, (block_count, 1))
    row_tags = row_ids[:, None]
    return jnp.where(
        row_tags > current, answer, jnp.where(row_tags == current, tiled, jnp.float32(0.0))
    )


def body(matrix, right_sides):
    row_count = lax.axis_size("row")
    row_index = lax.axis_index("row")
    col_index = lax.axis_index("col")
    block_size = NB
    local_rows = matrix.shape[0]
    block_count = local_rows // block_size
    row_ids = jnp.arange(local_rows) // block_size * row_count + row_index
    identity = jnp.eye(block_size, dtype=jnp.float32)
    work = matrix
    panels = []
    for current in range(PANELS):
        offset = current // row_count * block_size
        owner_row = current % row_count
        holder = col_index == current
        diag_local = jnp.where(
            holder, lax.slice_in_dim(work, offset, offset + block_size, axis=0), identity
        )
        column = jnp.where(holder, work, jnp.float32(0.0))
        diag_whole = broadcast(diag_local, "row", owner_row)
        factor = jnp.linalg.cholesky(diag_whole)
        local_panel = lower_panel(column, factor, row_ids, current, block_count)
        panel = broadcast(local_panel, "col", current)
        picked = col_index // row_count * block_size
        piece = lax.dynamic_slice_in_dim(panel, picked, block_size, 0)
        across = broadcast(piece, "row", col_index % row_count)
        update = jnp.dot(panel, across.T, precision=lax.Precision.HIGHEST)
        keeper = (row_ids[:, None] > current) & (col_index > current)
        work = jnp.where(keeper, work - update, work)
        panels.append(panel)
    factored = jnp.where(row_ids[:, None] < PANELS, jnp.float32(0.0), work)
    for current in range(PANELS):
        factored = jnp.where(col_index == current, panels[current], factored)
    rhs = right_sides
    for current in range(PANELS):
        offset = current // row_count * block_size
        owner_row = current % row_count
        diag_factor = jnp.where(
            row_index == owner_row,
            lax.slice_in_dim(panels[current], offset, offset + block_size, axis=0),
            identity,
        )
        local_rhs = lax.slice_in_dim(rhs, offset, offset + block_size, axis=0)
        answer = jax.scipy.linalg.solve_triangular(diag_factor, local_rhs, lower=True)
        shared = broadcast(answer, "row", owner_row)
        row_tags = row_ids[:, None]
        reduced = rhs - jnp.dot(panels[current], shared, precision=lax.Precision.HIGHEST)
        rhs = jnp.where(
            row_tags > current,
            reduced,
            jnp.where(row_tags == current, jnp.tile(shared, (block_count, 1)), rhs),
        )
    return (factored, rhs)


def solution(mesh):
    in_specs = (P("row", "col"), P("row", None))
    out_specs = (P("row", "col"), P("row", None))
    return jax.shard_map(body, mesh=mesh, in_specs=in_specs, out_specs=out_specs, check_vma=False)
```

profile of v0, /device:TPU:1, one launch (start us, length us, event | category | flops | bytes accessed | tf_op | source)
XLA Modules:
  0.0 1569.8 jit_solution(4977357209026958188)
XLA Ops:
  7.2 8.9 copy.8
  26.2 37.3 %all-reduce.10.cloned.1.call-done = f32[512,512]{0,1:T(8,128)} async-done(((f32[512,512]{0,1:T(8,128)}), f32[512,512]{0,1:T(8,128)}) %all-reduce.10.cloned.1.call-update) | async-done | bytes 1048592 | tf_op jit(solution)/shard_map/psum | solution.py:12
  66.5 11.7 cholesky.286
  78.4 9.8 custom-call.31
  88.9 11.7 cholesky.305
  100.7 10.0 custom-call.32
  111.4 11.7 cholesky.326
  123.1 9.8 custom-call.33
  133.5 22.3 %cholesky.343 = f32[128,128]{1,0:T(8,128)S(1)} custom-call(f32[128,128]{1,0:T(8,128)S(1)} %convolution_subtract_fusion.17), custom_call_target="Cholesky" | custom-call | tf_op jit(solution)/shard_map/jit(cholesky)/cholesky | solution.py:44
  169.3 39.3 %custom-call.34 = f32[4,128,128]{1,2,0:T(8,128)S(1)} custom-call(f32[4,128,128]{2,1,0:T(8,128)S(1)} %get-tuple-element.33), custom_call_target="InvertDiagBlocksLowerTriangular" | custom-call | tf_op jit(solution)/shard_map/jit(_solve_triangular)/triangular_solve | solution.py:16
  240.2 11.9 copy.21
  256.3 400.8 %all-reduce.12.cloned.1.call-done = f32[4096,512]{0,1:T(8,128)} async-done(((f32[4096,512]{0,1:T(8,128)}), f32[4096,512]{0,1:T(8,128)}) %all-reduce.12.cloned.1.call-update) | async-done | bytes 8388624 | tf_op jit(solution)/shard_map/psum | solution.py:12
  660.1 8.8 while.10
  668.9 39.3 %custom-call.39 = f32[4,128,128]{1,2,0:T(8,128)S(1)} custom-call(f32[4,128,128]{2,1,0:T(8,128)S(1)} %get-tuple-element.35), custom_call_target="InvertDiagBlocksLowerTriangular" | custom-call | tf_op jit(solution)/shard_map/jit(_solve_triangular)/triangular_solve | solution.py:67
  717.6 16.7 %subtract_select_fusion.1 = f32[4096,512]{0,1:T(8,128)S(1)} fusion(f32[4096,512]{0,1:T(8,128)} %copy.8, f32[4096,512]{0,1:T(8,128)} %all-reduce.12.cloned.1.call-done, f32[512,512]{0,1:T(8,128)} %all-reduce.14.cloned.1.call-done, pred[4096]{0:T(1024)(128)(4,1)S(1)} %broadcast_and_fusion.1), kind=kOutput, calls=%fused_computation.9 | convolution fusion | flops 12889096192 | bytes 26218496 | tf_op jit(solution)/shard_map/dot_general | solution.py:50
  743.4 57.9 %all-reduce.20.cloned.1.call-done = (f32[512,512]{0,1:T(8,128)}, f32[512,256]{1,0:T(8,128)}) async-done(((f32[512,512]{0,1:T(8,128)}, f32[512,256]{1,0:T(8,128)}), (f32[512,512]{0,1:T(8,128)}, f32[512,256]{1,0:T(8,128)})) %all-reduce.20.cloned.1.call-update) | async-done | bytes 1572880 | tf_op jit(solution)/shard_map/psum | solution.py:12
  804.3 11.7 cholesky.358
  816.2 9.8 custom-call.35
  826.7 11.7 cholesky.377
  838.4 10.2 custom-call.36
  849.3 11.7 cholesky.398
  861.1 9.8 custom-call.37
  871.5 11.9 cholesky.415
  897.5 39.3 %custom-call.38 = f32[4,128,128]{1,2,0:T(8,128)S(1)} custom-call(f32[4,128,128]{2,1,0:T(8,128)S(1)} %get-tuple-element.34), custom_call_target="InvertDiagBlocksLowerTriangular" | custom-call | tf_op jit(solution)/shard_map/jit(_solve_triangular)/triangular_solve | solution.py:16
  968.4 11.9 copy.22
  989.0 17.7 %fusion.19 = f32[4096,256]{1,0:T(8,128)} fusion(f32[4096,256]{1,0:T(8,128)S(1)} %bitcast_select_fusion.1, f32[4096,256]{1,0:T(8,128)S(1)} %copy-done.6, f32[4096,512]{0,1:T(8,128)} %all-reduce.12.cloned.1.call-done, f32[512,256]{1,0:T(8,128)S(1)} %copy-done.13, pred[4096]{0:T(1024)(128)(4,1)S(1)} %get-tuple-element.128), kind=kOutput, calls=%fused_computation.35 | convolution fusion | flops 6444548096 | bytes 21499904 | tf_op jit(solution)/shard_map/dot_general | solution.py:70
  1006.8 379.5 %all-reduce.16.cloned.1.call-done = f32[4096,512]{0,1:T(8,128)} async-done(((f32[4096,512]{0,1:T(8,128)}), f32[4096,512]{0,1:T(8,128)}) %all-reduce.16.cloned.1.call-update) | async-done | bytes 8388624 | tf_op jit(solution)/shard_map/psum | solution.py:12
  1397.9 39.3 %custom-call.40 = f32[4,128,128]{1,2,0:T(8,128)S(1)} custom-call(f32[4,128,128]{2,1,0:T(8,128)S(1)} %get-tuple-element.36), custom_call_target="InvertDiagBlocksLowerTriangular" | custom-call | tf_op jit(solution)/shard_map/jit(_solve_triangular)/triangular_solve | solution.py:67
  1444.2 64.7 %all-reduce.18.cloned.1.call-done = (f32[512,512]{0,1:T(8,128)}, f32[512,256]{1,0:T(8,128)}) async-done(((f32[512,512]{0,1:T(8,128)}, f32[512,256]{1,0:T(8,128)}), (f32[512,512]{0,1:T(8,128)}, f32[512,256]{1,0:T(8,128)})) %all-reduce.18.cloned.1.call-update) | async-done | bytes 1572880 | tf_op jit(solution)/shard_map/psum | solution.py:12
  1508.9 23.2 %fusion.2 = f32[4096,512]{0,1:T(8,128)} fusion(f32[4096,512]{0,1:T(8,128)} %all-reduce.16.cloned.1.call-done, f32[4096,512]{0,1:T(8,128)} %all-reduce.12.cloned.1.call-done, f32[4096,512]{0,1:T(8,128)} %copy-done, f32[512,512]{0,1:T(8,128)} %get-tuple-element.79, pred[4096]{0:T(1024)(128)(4,1)S(1)} %get-tuple-element.124, ...), kind=kOutput, calls=%fused_computation.12 | convolution fusion | flops 12895387648 | bytes 34611200 | tf_op jit(solution)/shard_map/dot_general | solution.py:50
  1532.1 9.0 copy.16
  1544.5 18.0 %fusion.20 = f32[4096,256]{1,0:T(8,128)} fusion(f32[4096,256]{1,0:T(8,128)S(1)} %bitcast_select_fusion, f32[4096,256]{1,0:T(8,128)S(1)} %copy-done.1, f32[4096,512]{0,1:T(8,128)} %all-reduce.16.cloned.1.call-done, f32[512,256]{1,0:T(8,128)S(1)} %copy-done.14, pred[4096]{0:T(1024)(128)(4,1)S(1)} %get-tuple-element.126), kind=kOutput, calls=%fused_computation.36 | convolution fusion | flops 6444548096 | bytes 21499904 | tf_op jit(solution)/shard_map/dot_general | solution.py:70
  (205 shorter events, 194.4 us)
Async XLA Ops:
  7.2 56.4 %all-reduce.10.cloned.1.call-start = ((), (), s32[]{:S(2)}) async-start(), calls=%async_computation | async-start | bytes 2097152 | tf_op jit(solution)/shard_map/psum | solution.py:12
  18.5 638.7 %all-reduce.12.cloned.1.call-start = ((), (), s32[]{:S(2)}) async-start(), calls=%async_computation.1 | async-start | bytes 16777216 | tf_op jit(solution)/shard_map/psum | solution.py:12
  217.6 6.7 copy-start.2
  224.3 6.7 copy-start.7
  240.2 11.9 copy-start.3
  240.2 11.9 copy-start.8
  240.2 11.9 copy-start.11
  256.2 461.4 %all-reduce.14.cloned.1.call-start = ((), (), s32[]{:S(2)}) async-start(), calls=%async_computation.2 | async-start | bytes 2097152 | tf_op jit(solution)/shard_map/psum | solution.py:12
  660.1 141.2 %all-reduce.20.cloned.1.call-start = ((), (), s32[]{:S(2)}) async-start(), calls=%async_computation.5 | async-start | bytes 3145728 | tf_op jit(solution)/shard_map/psum | solution.py:12
  734.3 3.4 copy-start
  738.9 647.4 %all-reduce.16.cloned.1.call-start = ((), (), s32[]{:S(2)}) async-start(), calls=%async_computation.3 | async-start | bytes 16777216 | tf_op jit(solution)/shard_map/psum | solution.py:12
  945.8 6.7 copy-start.4
  952.5 6.7 copy-start.9
  968.4 11.9 copy-start.5
  968.4 11.9 copy-start.10
  968.4 11.9 copy-start.12
  984.5 1.0 copy-start.13
  984.6 524.3 %all-reduce.18.cloned.1.call-start = ((), (), s32[]{:S(2)}) async-start(), calls=%async_computation.4 | async-start | bytes 3145728 | tf_op jit(solution)/shard_map/psum | solution.py:12
  985.6 3.4 copy-start.6
  1532.1 9.0 copy-start.14
  1541.1 3.4 copy-start.1
Sparse Core Ops, SparseCore 0:
  18.6 44.8 all-reduce.9
  256.3 400.7 all-reduce.11
  660.4 57.1 all-reduce.13
  739.0 62.2 all-reduce.19
  984.7 401.5 all-reduce.15
  1444.3 64.5 all-reduce.17
where the time goes:
time: 1580 us; the launch traced here: 1570 us
  waiting for transfers between devices  943 us (60%)
  other arithmetic  368 us (23%)
  matrix products  143 us (9%)
  local copies, waits for them, and re-layouts  95 us (6%)
  between operations  20.3 us (1%)
    psum x6, waiting for transfers between devices, broadcast(): return lax.psum(block, axis)  943 us
    another operation x29, other arithmetic, body(): factor = jnp.linalg.cholesky(diag_whole)  169 us
    another operation x4, other arithmetic, body(): jax.scipy.linalg.solve_triangular(diag_factor, local_rhs, lower=True)  84.5 us
    another operation x5, other arithmetic, lower_panel(): answer = jax.scipy.linalg.solve_triangular(factor, column.T, lower=True).T  81.2 us
    another operation x14, matrix products, lower_panel(): answer = jax.scipy.linalg.solve_triangular(factor, column.T, lower=True).T  51.2 us
    unnamed x34, local copies, waits for them, and re-layouts  47.5 us
    dot_general x2, matrix products, body(): update = jnp.dot(panel, across.T, precision=lax.Precision.HIGHEST)  39.9 us
    dot_general x2, matrix products, body(): jnp.dot(panels[current], shared, precision=lax.Precision.HIGHEST)  35.7 us
  transfers between devices with their start and end apart: 6, of which 6 were waited for; matrix products, arithmetic and copies ran while one was open for 6% of the time, Pallas kernels for 0%

commit v1 on v0

v1 whole, which is shorter than its diff:
```python
import functools
import jax
import jax.numpy as jnp
from jax import lax
from jax.experimental import pallas as pl
from jax.experimental.pallas import tpu as pltpu
from jax.sharding import PartitionSpec as P

NB = 512
EDGE = 1024
TILE = 128
AXES = ("row", "col")
F32 = jnp.float32
BF16 = jnp.bfloat16
NN = (((1,), (0,)), ((), ()))
NT = (((1,), (1,)), ((), ()))
VMEM = pl.BlockSpec(memory_space=pltpu.VMEM)


def device_index(x, y, z, core):
    return ((x % 2) * 2 + core) * 32 + (z % 4) * 8 + (y % 4) * 2 + (x % 4) // 2


def route(rule):
    pairs = []
    for x in range(4):
        for y in range(4):
            for z in range(4):
                for core in range(2):
                    target = rule(x, y, z, core)
                    if target is not None:
                        pairs.append((device_index(x, y, z, core), device_index(*target)))
    return pairs


def send(value, rule):
    return lax.ppermute(value, AXES, route(rule))


def swap_cores(value):
    return send(value, lambda x, y, z, c: (x, y, z, 1 - c))


def split(value):
    high = value.astype(BF16)
    return high, (value - high.astype(F32)).astype(BF16)


def dot3(a, b, dims=NN):
    ah, al = split(a)
    bh, bl = split(b)
    mul = lambda p, q: lax.dot_general(p, q, dims, preferred_element_type=F32)
    return mul(ah, bh) + (mul(ah, bl) + mul(al, bh))


def dot_full(a, b, dims=NN):
    return lax.dot_general(a, b, dims, precision=lax.Precision.HIGHEST, preferred_element_type=F32)


def factor_tile(work, inverse, factor_t):
    rows = lax.broadcasted_iota(jnp.int32, (TILE, TILE), 0)
    lanes = lax.broadcasted_iota(jnp.int32, (TILE, TILE), 1)
    inverse[...] = jnp.where(rows == lanes, F32(1), F32(0))
    lane8 = lax.broadcasted_iota(jnp.int32, (8, TILE), 1)

    def group(g, carry):
        top = work[0:8, :]
        cols = [jnp.broadcast_to(top[:, s : s + 1], (8, TILE)) for s in range(8)]
        e = [[cols[s][t : t + 1, :] if s <= t else None for s in range(8)] for t in range(8)]
        low = [[None] * 8 for _ in range(8)]
        scale = [None] * 8
        for s in range(8):
            r = lax.rsqrt(e[s][s])
            r = r * (F32(1.5) - F32(0.5) * e[s][s] * r * r)
            scale[s] = r
            for t in range(s + 1, 8):
                low[t][s] = e[t][s] * r
            for u in range(s + 1, 8):
                for t in range(u, 8):
                    e[t][u] = e[t][u] - low[t][s] * low[u][s]
        inv = [[None] * 8 for _ in range(8)]
        for s in range(8):
            inv[s][s] = scale[s]
            for t in range(s + 1, 8):
                total = low[t][s] * inv[s][s]
                for u in range(s + 1, t):
                    total = total + low[t][u] * inv[u][s]
                inv[t][s] = -total * scale[t]
        zero = jnp.zeros((1, TILE), F32)
        eye = inverse[pl.ds(pl.multiple_of(g * 8, 8), 8), :]
        upper = None
        solved = None
        for t in range(8):
            column = jnp.concatenate([inv[s][t] if s >= t else zero for s in range(8)], axis=0)
            a = column * top[t : t + 1, :]
            b = column * eye[t : t + 1, :]
            upper = a if upper is None else upper + a
            solved = b if solved is None else solved + b
        upper = jnp.where(lane8 < TILE - 8 * g, upper, F32(0))
        factor_t[pl.ds(pl.multiple_of(g * 8, 8), 8), :] = pltpu.roll(upper, 8 * g, 1)
        side = upper.T
        for q in range(1, 16):
            at = pl.ds(pl.multiple_of(((g + q) % 16) * 8, 8), 8)
            new = work[8 * q : 8 * q + 8, :]
            row = inverse[at, :]
            for s in range(8):
                mult = jnp.broadcast_to(side[8 * q : 8 * q + 8, s : s + 1], (8, TILE))
                new = new - mult * upper[s : s + 1, :]
                row = row - mult * solved[s : s + 1, :]
            work[8 * q - 8 : 8 * q, :] = pltpu.roll(new, TILE - 8, 1)
            inverse[at, :] = row
        inverse[pl.ds(pl.multiple_of(g * 8, 8), 8), :] = solved
        return carry

    lax.fori_loop(0, 16, group, 0)


def factor_kernel(a00, a10, a11, low, inv, inv_t, mat, work, tile_inv, tile_t):
    rows = lax.broadcasted_iota(jnp.int32, (TILE, TILE), 0)
    lanes = lax.broadcasted_iota(jnp.int32, (TILE, TILE), 1)
    mat[0:NB, 0:NB] = a00[...]
    mat[NB:EDGE, 0:NB] = a10[...]
    mat[NB:EDGE, NB:EDGE] = a11[...]
    low[...] = jnp.zeros_like(low)
    inv[...] = jnp.zeros_like(inv)
    inv_t[...] = jnp.zeros_like(inv_t)
    for b in range(EDGE // TILE):
        s, e = b * TILE, (b + 1) * TILE
        work[...] = mat[s:e, s:e]
        factor_tile(work, tile_inv, tile_t)
        x = jnp.where(rows >= lanes, tile_inv[...], F32(0))
        low[s:e, s:e] = jnp.where(rows >= lanes, tile_t[...].T, F32(0))
        inv[s:e, s:e] = x
        inv_t[s:e, s:e] = x.T
        if b > 0:
            left = dot_full(low[s:e, 0:s], inv[0:s, 0:s])
            left = -dot_full(x, left)
            inv[s:e, 0:s] = left
            inv_t[0:s, s:e] = left.T
        if e < EDGE:
            panel = dot_full(mat[e:EDGE, s:e], x, NT)
            low[e:EDGE, s:e] = panel
            for c in range(e, EDGE, 2 * TILE):
                d = min(c + 2 * TILE, EDGE)
                mat[c:EDGE, c:d] = mat[c:EDGE, c:d] - dot_full(panel[c - e :], panel[c - e : d - e], NT)


def solve_kernel(col_ref, g0, g1, inv, inv_t, wh, wl, y, mid):
    col = col_ref[0]
    step = 256
    for b in range(EDGE // step):
        s, e = b * step, (b + 1) * step
        if e <= NB:
            part = dot3(inv[s:e, 0:e], g0[0:e, :])
        else:
            part = dot3(inv[s:e, 0:NB], g0[...]) + dot3(inv[s:e, NB:e], g1[0 : e - NB, :])
        y[s:e, :] = part[:, NB:]
        mid[s:e, NB:] = part[:, NB:]
        rows = lax.broadcasted_iota(jnp.int32, (step, NB), 0) + s
        lanes = lax.broadcasted_iota(jnp.int32, (step, NB), 1) + col * NB
        mid[s:e, 0:NB] = jnp.where(col < 2, jnp.where(rows == lanes, F32(-1), F32(0)), part[:, 0:NB])
    for b in range(EDGE // step):
        s, e = b * step, (b + 1) * step
        h, l = split(dot3(inv_t[s:e, s:EDGE], mid[s:EDGE, :]))
        wh[s:e, :] = h
        wl[s:e, :] = l


def update_kernel(place, rows_ref, wh, wl, mat, rhs, special, y, out, out_rhs):
    step = pl.program_id(0)
    row, col = place[0], place[1]
    rh, rl = split(rows_ref[...])
    mul = lambda p, q: lax.dot_general(p, q, NN, preferred_element_type=F32)
    acc = mul(rh, wh[...]) + (mul(rh, wl[...]) + mul(rl, wh[...]))
    base = jnp.where(col < 2, F32(0), mat[...])
    out[...] = base - acc[:, 0:NB]
    out_rhs[...] = rhs[...] - acc[:, NB:]

    @pl.when(jnp.logical_and(step == 0, row < 2))
    def _():
        out[...] = special[...]
        out_rhs[...] = y[...]


def ordered(parts, first):
    both = jnp.concatenate(parts + parts, axis=0)
    size = parts[0].shape[0]
    return lax.dynamic_slice_in_dim(both, (4 - first) % 4 * size, 4 * size, 0)


def spread_leading(block, z, y):
    at_origin = lambda f: (lambda X, Y, Z, C: f(X, Y, Z, C) if (X, Y, Z) == (0, 0, 0) else None)
    part = block.shape[0] // 4
    got = jnp.where(z == 0, block[0:part], F32(0))
    for d in (1, 2, 3):
        got = got + send(block[d * part : (d + 1) * part], at_origin(lambda X, Y, Z, C, d=d: (0, 0, d, C)))
    small = part // 4
    mine = jnp.where(y == 0, got[0:small], F32(0))
    for d in (1, 2, 3):
        mine = mine + send(
            got[d * small : (d + 1) * small], lambda X, Y, Z, C, d=d: (0, d, Z, C) if (X, Y) == (0, 0) else None
        )
    x = lax.axis_index("col") % 2 * 2 + lax.axis_index("row") // 2
    all_x = jnp.where(x == 0, mine, F32(0))
    for d in (1, 2, 3):
        all_x = all_x + send(mine, lambda X, Y, Z, C, d=d: (d, Y, Z, C) if X == 0 else None)
    ring_y = ordered([all_x] + [send(all_x, lambda X, Y, Z, C, d=d: (X, Y - d, Z, C)) for d in (1, 2, 3)], y)
    return ordered([ring_y] + [send(ring_y, lambda X, Y, Z, C, d=d: (X, Y, Z - d, C)) for d in (1, 2, 3)], z)


def body(matrix, right_sides):
    row = lax.axis_index("row")
    col = lax.axis_index("col")
    core, x_lo = row % 2, row // 2
    z, y = col // 8, col // 2 % 4
    first = matrix[0:NB]

    corner = send(first, lambda X, Y, Z, C: (0, 0, 0, 0) if (X, Y, Z, C) == (2, 0, 0, 1) else None)
    corner2 = swap_cores(corner[NB // 2 :])
    extra = jnp.where(core == 0, corner[0 : NB // 2], corner2)
    leading = spread_leading(jnp.concatenate([first, extra], axis=0), z, y)
    other = swap_cores(leading)
    lead0 = jnp.where(core == 0, leading, other)
    lead1 = jnp.where(core == 0, other, leading)
    a00, a10 = lead0[0:NB], lead1[0:NB]
    a11 = jnp.concatenate([lead0[NB:], lead1[NB:]], axis=0)

    top = jnp.concatenate([first, right_sides[0:NB]], axis=1)
    crossed = send(top, lambda X, Y, Z, C: (X + 1, Y, Z, C) if X % 2 == 0 else None)
    own = jnp.where(x_lo == 0, top, crossed)
    partner = swap_cores(own)
    g0 = jnp.where(core == 0, own, partner)
    g1 = jnp.where(core == 0, partner, own)

    rows_t = jnp.concatenate([g0[:, 0:NB].T, g1[:, 0:NB].T], axis=1)
    quarter = lambda t: lax.dynamic_slice_in_dim(rows_t, t * TILE, TILE, 0)
    piece = jnp.where(col % 4 == row, quarter(row), F32(0))
    for s in (1, 2, 3):

        def rule(X, Y, Z, C, s=s):
            r = (X % 2) * 2 + C
            t = (Y % 2) * 2 + X // 2
            if t != r:
                return None
            t = r ^ s
            return (X % 2 + 2 * (t % 2), Y // 2 * 2 + t // 2, Z, C)

        piece = piece + send(quarter(jnp.bitwise_xor(row, s)), rule)
    panel_rows = lax.all_gather(piece, "col", axis=0, tiled=True)

    square = jax.ShapeDtypeStruct((EDGE, EDGE), F32)
    low, inv, inv_t = pl.pallas_call(
        factor_kernel,
        out_shape=(square, square, square),
        in_specs=[VMEM] * 3,
        out_specs=(VMEM,) * 3,
        scratch_shapes=[
            pltpu.VMEM((EDGE, EDGE), F32),
            pltpu.VMEM((TILE, TILE), F32),
            pltpu.VMEM((TILE, TILE), F32),
            pltpu.VMEM((TILE, TILE), F32),
        ],
        compiler_params=pltpu.CompilerParams(vmem_limit_bytes=48 << 20),
        cost_estimate=pl.CostEstimate(flops=100_000_000_000, bytes_accessed=16 << 20, transcendentals=0),
        name="factor",
    )(a00, a10, a11)

    width = NB + right_sides.shape[1]
    wh, wl, answer = pl.pallas_call(
        solve_kernel,
        out_shape=(
            jax.ShapeDtypeStruct((EDGE, width), BF16),
            jax.ShapeDtypeStruct((EDGE, width), BF16),
            jax.ShapeDtypeStruct((EDGE, width - NB), F32),
        ),
        in_specs=[pl.BlockSpec(memory_space=pltpu.SMEM)] + [VMEM] * 4,
        out_specs=(VMEM,) * 3,
        scratch_shapes=[pltpu.VMEM((EDGE, width), F32)],
        compiler_params=pltpu.CompilerParams(vmem_limit_bytes=48 << 20),
        cost_estimate=pl.CostEstimate(flops=10_000_000_000, bytes_accessed=16 << 20, transcendentals=0),
        name="solve",
    )(col.reshape(1), g0, g1, inv, inv_t)

    at = row % 2 * NB
    lower = lax.dynamic_slice(low, (at, col % 2 * NB), (NB, NB))
    special = jnp.where(col < 2, lower, F32(0))
    answer = lax.dynamic_slice_in_dim(answer, at, NB, 0)

    blocks = matrix.shape[0] // NB
    grid_spec = pltpu.PrefetchScalarGridSpec(
        num_scalar_prefetch=1,
        grid=(blocks,),
        in_specs=[
            pl.BlockSpec((NB, EDGE), lambda i, place: (i, 0)),
            pl.BlockSpec((EDGE, width), lambda i, place: (0, 0)),
            pl.BlockSpec((EDGE, width), lambda i, place: (0, 0)),
            pl.BlockSpec((NB, NB), lambda i, place: (i, 0)),
            pl.BlockSpec((NB, width - NB), lambda i, place: (i, 0)),
            pl.BlockSpec((NB, NB), lambda i, place: (0, 0)),
            pl.BlockSpec((NB, width - NB), lambda i, place: (0, 0)),
        ],
        out_specs=[
            pl.BlockSpec((NB, NB), lambda i, place: (i, 0)),
            pl.BlockSpec((NB, width - NB), lambda i, place: (i, 0)),
        ],
    )
    return pl.pallas_call(
        update_kernel,
        grid_spec=grid_spec,
        out_shape=(
            jax.ShapeDtypeStruct(matrix.shape, F32),
            jax.ShapeDtypeStruct(right_sides.shape, F32),
        ),
        compiler_params=pltpu.CompilerParams(vmem_limit_bytes=56 << 20),
        cost_estimate=pl.CostEstimate(flops=20_000_000_000, bytes_accessed=44 << 20, transcendentals=0),
        name="update",
    )(jnp.stack([row, col]), panel_rows, wh, wl, matrix, right_sides, special, answer)


def solution(mesh):
    specs = (P("row", "col"), P("row", None))
    return jax.shard_map(body, mesh=mesh, in_specs=specs, out_specs=specs, check_vma=False)
```

time: 1580 us -> 462 us (0.29)
  waiting for transfers between devices: 943 us -> 191 us
  other arithmetic: 368 us -> 15.8 us
  Pallas kernels: 0 us -> 147 us
  matrix products: 143 us -> 0 us
  local copies, waits for them, and re-layouts: 95 us -> 32.7 us
  starting transfers between devices: 0.46 us -> 59 us
    psum x6 -> x0, waiting for transfers between devices: 943 us -> none  [broadcast(): return lax.psum(block, axis)]
    another operation x38 -> x1, other arithmetic: 334 us -> 0.55 us  [body(): jnp.stack([row, col])]
    ppermute x0 -> x23, waiting for transfers between devices: none -> 191 us  [send(): return lax.ppermute(value, AXES, route(rule))]
    pallas_call x0 -> x3, Pallas kernels: none -> 147 us  [the longest x1 109 us: body(): pl.pallas_call(factor_kernel, out_shape=(square, square, square), in_spec...]
    dot_general x4 -> x0, matrix products: 75.5 us -> none  [the longest x2 39.9 us: body(): update = jnp.dot(panel, across.T, precision=lax.Precision.HIGHEST)]
    another operation x40 -> x0, matrix products: 67.1 us -> none  [the longest x14 51.2 us: lower_panel(): answer = jax.scipy.linalg.solve_triangular(factor, column.T, lower=True).T]
    ppermute x0 -> x23, starting transfers between devices: none -> 59 us  [send(): return lax.ppermute(value, AXES, route(rule))]
    another operation x79 -> x0, local copies, waits for them, and re-layouts: 41.3 us -> none  [the longest x40 17 us: body(): jax.scipy.linalg.solve_triangular(diag_factor, local_rhs, lower=True)]
  transfers between devices with their start and end apart: 6 -> 24, of which waited for: 6 -> 16; matrix products, arithmetic and copies ran while one was open for 6% -> 7% of each run, Pallas kernels for 0% -> 26%
where the time goes in v1:
time: 462 us; the launch traced here: 460 us
  waiting for transfers between devices  191 us (41%)
  Pallas kernels  147 us (32%)
  starting transfers between devices  59 us (13%)
  local copies, waits for them, and re-layouts  32.7 us (7%)
  other arithmetic  15.8 us (3%)
  between operations  14.6 us (3%)
    ppermute x23, waiting for transfers between devices, send(): return lax.ppermute(value, AXES, route(rule))  191 us
    pallas_call x1, Pallas kernels, body(): pl.pallas_call(factor_kernel, out_shape=(square, square, square), in_spec...  109 us
    ppermute x23, starting transfers between devices, send(): return lax.ppermute(value, AXES, route(rule))  59 us
    pallas_call x1, Pallas kernels, body(): pl.pallas_call(update_kernel, grid_spec=grid_spec, out_shape=(jax.ShapeDt...  26.9 us
    pallas_call x1, Pallas kernels, body(): pl.pallas_call(solve_kernel, out_shape=(jax.ShapeDtypeStruct((EDGE, width...  11.5 us
  transfers between devices with their start and end apart: 24, of which 16 were waited for; matrix products, arithmetic and copies ran while one was open for 7% of the time, Pallas kernels for 26%

profile of v1, /device:TPU:1, one launch (start us, length us, event | category | flops | bytes accessed | tf_op | source)
XLA Modules:
  0.0 460.1 jit_solution(11763124012211540536)
XLA Ops:
  9.8 5.1 %collective-permute-start = (f32[512,768]{0,1:T(8,128)S(1)}, f32[512,768]{0,1:T(8,128)}, u32[]{:S(2)}, u32[]{:S(2)}) collective-permute-start(f32[512,768]{0,1:T(8,128)S(1)} %pad_maximum_fusion), channel_id=1, source_target_pairs={{0,64},{32,96},{8,72},{40,104},{16,80},{48,112},{24,88},{56,120},{... | collective-permute-start | bytes 4718600 | tf_op jit(solution)/shard_map/ppermute | solution.py:37
  14.9 31.9 %collective-permute-done = f32[512,768]{0,1:T(8,128)} collective-permute-done((f32[512,768]{0,1:T(8,128)S(1)}, f32[512,768]{0,1:T(8,128)}, u32[]{:S(2)}, u32[]{:S(2)}) %collective-permute-start) | collective-permute-done | bytes 1572896 | tf_op jit(solution)/shard_map/ppermute | solution.py:37
  48.7 3.2 collective-permute-done.1
  60.8 7.5 %collective-permute-done.2 = f32[128,1024]{1,0:T(8,128)} collective-permute-done((f32[128,1024]{1,0:T(8,128)}, f32[128,1024]{1,0:T(8,128)}, u32[]{:S(2)}, u32[]{:S(2)}) %collective-permute-start.2) | collective-permute-done | bytes 524320 | tf_op jit(solution)/shard_map/ppermute | solution.py:37
  68.3 2.3 fusion.5
  72.2 24.8 %collective-permute-start.7 = (f32[256,512]{0,1:T(8,128)}, f32[256,512]{0,1:T(8,128)}, u32[]{:S(2)}, u32[]{:S(2)}) collective-permute-start(f32[256,512]{0,1:T(8,128)} %slice.77), channel_id=1, source_target_pairs={{0,32},{32,0},{8,40},{40,8},{16,48},{48,16},{24,56},{56,24},{2,34}... | collective-permute-start | bytes 1572872 | tf_op jit(solution)/shard_map/ppermute | solution.py:37
  98.4 2.1 collective-permute-start.5
  103.9 2.1 collective-permute-start.9
  106.2 8.7 %collective-permute-done.5 = f32[192,512]{0,1:T(8,128)} collective-permute-done((f32[192,512]{0,1:T(8,128)S(1)}, f32[192,512]{0,1:T(8,128)}, u32[]{:S(2)}, u32[]{:S(2)}) %collective-permute-start.5) | collective-permute-done | bytes 393248 | tf_op jit(solution)/shard_map/ppermute | solution.py:37
  114.9 20.8 %collective-permute-done.8 = f32[192,512]{0,1:T(8,128)S(1)} collective-permute-done((f32[192,512]{0,1:T(8,128)}, f32[192,512]{0,1:T(8,128)S(1)}, u32[]{:S(2)}, u32[]{:S(2)}) %collective-permute-start.8) | collective-permute-done | bytes 393248 | tf_op jit(solution)/shard_map/ppermute | solution.py:37
  141.5 3.5 collective-permute-done.10
  144.9 5.6 %collective-permute-done.11 = f32[48,512]{0,1:T(8,128)S(1)} collective-permute-done((f32[48,512]{0,1:T(8,128)S(1)}, f32[48,512]{0,1:T(8,128)S(1)}, u32[]{:S(2)}, u32[]{:S(2)}) %collective-permute-start.11) | collective-permute-done | bytes 98336 | tf_op jit(solution)/shard_map/ppermute | solution.py:37
  154.6 5.4 %collective-permute-done.13 = f32[48,512]{0,1:T(8,128)S(1)} collective-permute-done((f32[48,512]{0,1:T(8,128)S(1)}, f32[48,512]{0,1:T(8,128)S(1)}, u32[]{:S(2)}, u32[]{:S(2)}) %collective-permute-start.13) | collective-permute-done | bytes 98336 | tf_op jit(solution)/shard_map/ppermute | solution.py:37
  160.0 11.2 %collective-permute-done.14 = f32[48,512]{0,1:T(8,128)S(1)} collective-permute-done((f32[48,512]{0,1:T(8,128)S(1)}, f32[48,512]{0,1:T(8,128)S(1)}, u32[]{:S(2)}, u32[]{:S(2)}) %collective-permute-start.14) | collective-permute-done | bytes 98336 | tf_op jit(solution)/shard_map/ppermute | solution.py:37
  171.2 48.9 %collective-permute-done.15 = f32[48,512]{0,1:T(8,128)S(1)} collective-permute-done((f32[48,512]{0,1:T(8,128)S(1)}, f32[48,512]{0,1:T(8,128)S(1)}, u32[]{:S(2)}, u32[]{:S(2)}) %collective-permute-start.15) | collective-permute-done | bytes 98336 | tf_op jit(solution)/shard_map/ppermute | solution.py:37
  220.3 3.7 collective-permute-start.17
  224.7 9.1 %collective-permute-done.16 = f32[48,512]{0,1:T(8,128)S(1)} collective-permute-done((f32[48,512]{0,1:T(8,128)S(1)}, f32[48,512]{0,1:T(8,128)S(1)}, u32[]{:S(2)}, u32[]{:S(2)}) %collective-permute-start.16) | collective-permute-done | bytes 98336 | tf_op jit(solution)/shard_map/ppermute | solution.py:37
  233.8 2.4 collective-permute-done.17
  236.2 10.4 %collective-permute-done.18 = f32[48,512]{0,1:T(8,128)S(1)} collective-permute-done((f32[48,512]{0,1:T(8,128)S(1)}, f32[48,512]{0,1:T(8,128)S(1)}, u32[]{:S(2)}, u32[]{:S(2)}) %collective-permute-start.18) | collective-permute-done | bytes 98336 | tf_op jit(solution)/shard_map/ppermute | solution.py:37
  247.8 3.0 collective-permute-start.20
  251.6 8.3 %collective-permute-done.19 = f32[192,512]{0,1:T(8,128)S(1)} collective-permute-done((f32[192,512]{0,1:T(8,128)S(1)}, f32[192,512]{0,1:T(8,128)S(1)}, u32[]{:S(2)}, u32[]{:S(2)}) %collective-permute-start.19) | collective-permute-done | bytes 393248 | tf_op jit(solution)/shard_map/ppermute | solution.py:37
  262.3 12.2 %collective-permute-done.21 = f32[192,512]{0,1:T(8,128)} collective-permute-done((f32[192,512]{0,1:T(8,128)S(1)}, f32[192,512]{0,1:T(8,128)}, u32[]{:S(2)}, u32[]{:S(2)}) %collective-permute-start.21) | collective-permute-done | bytes 393248 | tf_op jit(solution)/shard_map/ppermute | solution.py:37
  274.6 3.8 concatenate.22
  278.4 2.0 constant_dynamic-slice_fusion.1
  281.9 2.0 copy.11.g0
  285.5 2.4 broadcast_select_fusion
  292.9 2.5 copy.8.a00
  295.5 2.5 copy.9.a10
  300.4 108.8 %factor.1 = (f32[1024,1024]{1,0:T(8,128)}, f32[1024,1024]{1,0:T(8,128)}, f32[1024,1024]{1,0:T(8,128)}) custom-call(f32[512,512]{1,0:T(8,128)S(1)} %copy-done, f32[512,512]{1,0:T(8,128)S(1)} %copy-done.1, f32[512,512]{1,0:T(8,128)S(1)} %copy.10.a11), custom_call_target="tpu_custom_call" | custom-call | flops 99999997952 | bytes 16777216 | tf_op jit(solution)/shard_map/factor/pallas_call | solution.py:252
  409.2 11.5 %solve.1 = (bf16[1024,768]{1,0:T(8,128)(2,1)S(1)}, bf16[1024,768]{1,0:T(8,128)(2,1)S(1)}, f32[1024,256]{1,0:T(8,128)S(1)}) custom-call(s32[1]{0:T(128)} %bitcast.1.col_ref, f32[512,768]{1,0:T(8,128)S(1)} %copy.11.g0, f32[512,768]{1,0:T(8,128)} %copy.12.g1, f32[1024,1024]{1,0:T(8,128)} %get-tuple-element.8.inv, f32[1024,1024]{1,0:T(8,128)} %get-tuple-element.9.inv_t), custom_call_target="tpu_custom_call" | custom-call | flops 10000000000 | bytes 16777216 | tf_op jit(solution)/shard_map/solve/pallas_call | solution.py:269
  423.9 2.3 dynamic-slice_select_fusion.special
  426.2 26.9 %update.1 = (f32[4096,512]{1,0:T(8,128)}, f32[4096,256]{1,0:T(8,128)}) custom-call(s32[2]{0:T(128)} %pad_add_fusion.place, f32[4096,1024]{1,0:T(8,128)} %all-gather.2.cloned.1.call-done.rows_ref, bf16[1024,768]{1,0:T(8,128)(2,1)} %copy-done.2, bf16[1024,768]{1,0:T(8,128)(2,1)} %copy-done.3, f32[4096,512]{1,0:T(8,128)} %mat.1, f32[4096,256]{1,0:T(8,128)} %rhs.1, ...), custom_call_target="tpu_custom_call" | custom-call | flops 20000000000 | bytes 46137344 | tf_op jit(solution)/shard_map/update/pallas_call | solution.py:307
  (82 shorter events, 48.4 us)
Async XLA Ops:
  7.2 1.2 slice-start
  7.2 419.0 %all-gather.2.cloned.1.call-start = ((), (), s32[]{:S(2)}) async-start(), calls=%async_computation | async-start | bytes 17301504 | tf_op jit(solution)/shard_map/all_gather | solution.py:249
  9.8 37.0 %collective-permute-start = (f32[512,768]{0,1:T(8,128)S(1)}, f32[512,768]{0,1:T(8,128)}, u32[]{:S(2)}, u32[]{:S(2)}) collective-permute-start(f32[512,768]{0,1:T(8,128)S(1)} %pad_maximum_fusion), channel_id=1, source_target_pairs={{0,64},{32,96},{8,72},{40,104},{16,80},{48,112},{24,88},{56,120},{... | collective-permute-start | bytes 4718600 | tf_op jit(solution)/shard_map/ppermute | solution.py:37
  47.1 4.8 %collective-permute-start.1 = (f32[512,768]{0,1:T(8,128)S(1)}, f32[512,768]{0,1:T(8,128)}, u32[]{:S(2)}, u32[]{:S(2)}) collective-permute-start(f32[512,768]{0,1:T(8,128)S(1)} %broadcast_select_fusion.2), channel_id=1, source_target_pairs={{0,32},{32,0},{8,40},{40,8},{16,48},{48,16},{24,56},{56,24},{2,34}... | collective-permute-start | bytes 4718600 | tf_op jit(solution)/shard_map/ppermute | solution.py:37
  53.7 1.7 copy-start.7
  56.5 11.7 %collective-permute-start.2 = (f32[128,1024]{1,0:T(8,128)}, f32[128,1024]{1,0:T(8,128)}, u32[]{:S(2)}, u32[]{:S(2)}) collective-permute-start(f32[128,1024]{1,0:T(8,128)} %get-tuple-element.20), channel_id=1, source_target_pairs={{0,1},{8,9},{16,17},{24,25},{4,5},{12,13},{20,21},{28,29},{66,67},... | collective-permute-start | bytes 1572872 | tf_op jit(solution)/shard_map/ppermute | solution.py:37
  57.8 10.4 %collective-permute-start.3 = (f32[128,1024]{1,0:T(8,128)}, f32[128,1024]{1,0:T(8,128)}, u32[]{:S(2)}, u32[]{:S(2)}) collective-permute-start(f32[128,1024]{1,0:T(8,128)} %get-tuple-element.21), channel_id=1, source_target_pairs={{0,2},{8,10},{16,18},{24,26},{4,6},{12,14},{20,22},{28,30},{66,64}... | collective-permute-start | bytes 1572872 | tf_op jit(solution)/shard_map/ppermute | solution.py:37
  59.3 9.0 %collective-permute-start.4 = (f32[128,1024]{1,0:T(8,128)}, f32[128,1024]{1,0:T(8,128)}, u32[]{:S(2)}, u32[]{:S(2)}) collective-permute-start(f32[128,1024]{1,0:T(8,128)} %get-tuple-element.22), channel_id=1, source_target_pairs={{0,3},{8,11},{16,19},{24,27},{4,7},{12,15},{20,23},{28,31},{66,65}... | collective-permute-start | bytes 1572872 | tf_op jit(solution)/shard_map/ppermute | solution.py:37
  70.6 0.7 collective-permute-start.6
  72.2 28.3 %collective-permute-start.7 = (f32[256,512]{0,1:T(8,128)}, f32[256,512]{0,1:T(8,128)}, u32[]{:S(2)}, u32[]{:S(2)}) collective-permute-start(f32[256,512]{0,1:T(8,128)} %slice.77), channel_id=1, source_target_pairs={{0,32},{32,0},{8,40},{40,8},{16,48},{48,16},{24,56},{56,24},{2,34}... | collective-permute-start | bytes 1572872 | tf_op jit(solution)/shard_map/ppermute | solution.py:37
  98.4 16.5 %collective-permute-start.5 = (f32[192,512]{0,1:T(8,128)S(1)}, f32[192,512]{0,1:T(8,128)}, u32[]{:S(2)}, u32[]{:S(2)}) collective-permute-start(f32[192,512]{0,1:T(8,128)S(1)} %copy.16), channel_id=1, source_target_pairs={{0,8},{32,40}} | collective-permute-start | bytes 1179656 | tf_op jit(solution)/shard_map/ppermute | solution.py:37
  102.6 33.1 %collective-permute-start.8 = (f32[192,512]{0,1:T(8,128)}, f32[192,512]{0,1:T(8,128)S(1)}, u32[]{:S(2)}, u32[]{:S(2)}) collective-permute-start(f32[192,512]{0,1:T(8,128)} %get-tuple-element.26), channel_id=1, source_target_pairs={{0,16},{32,48}} | collective-permute-start | bytes 1179656 | tf_op jit(solution)/shard_map/ppermute | solution.py:37
  103.9 31.8 %collective-permute-start.9 = (f32[192,512]{0,1:T(8,128)S(1)}, f32[192,512]{0,1:T(8,128)}, u32[]{:S(2)}, u32[]{:S(2)}) collective-permute-start(f32[192,512]{0,1:T(8,128)S(1)} %get-tuple-element.27), channel_id=1, source_target_pairs={{0,24},{32,56}} | collective-permute-start | bytes 1179656 | tf_op jit(solution)/shard_map/ppermute | solution.py:37
  137.5 7.4 %collective-permute-start.10 = (f32[48,512]{0,1:T(8,128)S(1)}, f32[48,512]{0,1:T(8,128)S(1)}, u32[]{:S(2)}, u32[]{:S(2)}) collective-permute-start(f32[48,512]{0,1:T(8,128)S(1)} %get-tuple-element.23), channel_id=1, source_target_pairs={{0,2},{32,34},{8,10},{40,42},{16,18},{48,50},{24,26},{56,58}} | collective-permute-start | bytes 294920 | tf_op jit(solution)/shard_map/ppermute | solution.py:37
  138.8 11.7 %collective-permute-start.11 = (f32[48,512]{0,1:T(8,128)S(1)}, f32[48,512]{0,1:T(8,128)S(1)}, u32[]{:S(2)}, u32[]{:S(2)}) collective-permute-start(f32[48,512]{0,1:T(8,128)S(1)} %get-tuple-element.25), channel_id=1, source_target_pairs={{0,4},{32,36},{8,12},{40,44},{16,20},{48,52},{24,28},{56,60}} | collective-permute-start | bytes 294920 | tf_op jit(solution)/shard_map/ppermute | solution.py:37
  140.1 10.4 %collective-permute-start.12 = (f32[48,512]{0,1:T(8,128)S(1)}, f32[48,512]{0,1:T(8,128)S(1)}, u32[]{:S(2)}, u32[]{:S(2)}) collective-permute-start(f32[48,512]{0,1:T(8,128)S(1)} %get-tuple-element.24), channel_id=1, source_target_pairs={{0,6},{32,38},{8,14},{40,46},{16,22},{48,54},{24,30},{56,62}} | collective-permute-start | bytes 294920 | tf_op jit(solution)/shard_map/ppermute | solution.py:37
  150.6 9.4 %collective-permute-start.13 = (f32[48,512]{0,1:T(8,128)S(1)}, f32[48,512]{0,1:T(8,128)S(1)}, u32[]{:S(2)}, u32[]{:S(2)}) collective-permute-start(f32[48,512]{0,1:T(8,128)S(1)} %fusion.10), channel_id=1, source_target_pairs={{0,64},{32,96},{8,72},{40,104},{16,80},{48,112},{24,88},{56,120},{... | collective-permute-start | bytes 294920 | tf_op jit(solution)/shard_map/ppermute | solution.py:37
  151.9 19.3 %collective-permute-start.14 = (f32[48,512]{0,1:T(8,128)S(1)}, f32[48,512]{0,1:T(8,128)S(1)}, u32[]{:S(2)}, u32[]{:S(2)}) collective-permute-start(f32[48,512]{0,1:T(8,128)S(1)} %fusion.10), channel_id=1, source_target_pairs={{0,1},{32,33},{8,9},{40,41},{16,17},{48,49},{24,25},{56,57},{2,3},... | collective-permute-start | bytes 294920 | tf_op jit(solution)/shard_map/ppermute | solution.py:37
  153.2 66.9 %collective-permute-start.15 = (f32[48,512]{0,1:T(8,128)S(1)}, f32[48,512]{0,1:T(8,128)S(1)}, u32[]{:S(2)}, u32[]{:S(2)}) collective-permute-start(f32[48,512]{0,1:T(8,128)S(1)} %fusion.10), channel_id=1, source_target_pairs={{0,65},{32,97},{8,73},{40,105},{16,81},{48,113},{24,89},{56,121},{... | collective-permute-start | bytes 294920 | tf_op jit(solution)/shard_map/ppermute | solution.py:37
  220.2 13.6 %collective-permute-start.16 = (f32[48,512]{0,1:T(8,128)S(1)}, f32[48,512]{0,1:T(8,128)S(1)}, u32[]{:S(2)}, u32[]{:S(2)}) collective-permute-start(f32[48,512]{0,1:T(8,128)S(1)} %add_add_fusion.1), channel_id=1, source_target_pairs={{0,6},{32,38},{8,14},{40,46},{16,22},{48,54},{24,30},{56,62},{2,0}... | collective-permute-start | bytes 294920 | tf_op jit(solution)/shard_map/ppermute | solution.py:37
  220.3 15.9 %collective-permute-start.17 = (f32[48,512]{0,1:T(8,128)S(1)}, f32[48,512]{0,1:T(8,128)S(1)}, u32[]{:S(2)}, u32[]{:S(2)}) collective-permute-start(f32[48,512]{0,1:T(8,128)S(1)} %add_add_fusion.1), channel_id=1, source_target_pairs={{0,4},{32,36},{8,12},{40,44},{16,20},{48,52},{24,28},{56,60},{2,6}... | collective-permute-start | bytes 294920 | tf_op jit(solution)/shard_map/ppermute | solution.py:37
  224.0 22.6 %collective-permute-start.18 = (f32[48,512]{0,1:T(8,128)S(1)}, f32[48,512]{0,1:T(8,128)S(1)}, u32[]{:S(2)}, u32[]{:S(2)}) collective-permute-start(f32[48,512]{0,1:T(8,128)S(1)} %add_add_fusion.1), channel_id=1, source_target_pairs={{0,2},{32,34},{8,10},{40,42},{16,18},{48,50},{24,26},{56,58},{2,4}... | collective-permute-start | bytes 294920 | tf_op jit(solution)/shard_map/ppermute | solution.py:37
  247.7 13.8 %copy-start.8 = (f32[192,512]{0,1:T(8,128)}, f32[192,512]{0,1:T(8,128)S(1)}, u32[]{:S(2)}) copy-start(f32[192,512]{0,1:T(8,128)S(1)} %constant_dynamic-slice_fusion.2) | copy-start | bytes 1179652
  247.7 12.2 %collective-permute-start.19 = (f32[192,512]{0,1:T(8,128)S(1)}, f32[192,512]{0,1:T(8,128)S(1)}, u32[]{:S(2)}, u32[]{:S(2)}) collective-permute-start(f32[192,512]{0,1:T(8,128)S(1)} %constant_dynamic-slice_fusion.2), channel_id=1, source_target_pairs={{0,24},{32,56},{8,0},{40,32},{16,8},{48,40},{24,16},{56,48},{2,26}... | collective-permute-start | bytes 1179656 | tf_op jit(solution)/shard_map/ppermute | solution.py:37
  247.8 13.7 %collective-permute-start.20 = (f32[192,512]{0,1:T(8,128)S(1)}, f32[192,512]{0,1:T(8,128)S(1)}, u32[]{:S(2)}, u32[]{:S(2)}) collective-permute-start(f32[192,512]{0,1:T(8,128)S(1)} %constant_dynamic-slice_fusion.2), channel_id=1, source_target_pairs={{0,16},{32,48},{8,24},{40,56},{16,0},{48,32},{24,8},{56,40},{2,18}... | collective-permute-start | bytes 1179656 | tf_op jit(solution)/shard_map/ppermute | solution.py:37
  250.8 23.8 %collective-permute-start.21 = (f32[192,512]{0,1:T(8,128)S(1)}, f32[192,512]{0,1:T(8,128)}, u32[]{:S(2)}, u32[]{:S(2)}) collective-permute-start(f32[192,512]{0,1:T(8,128)S(1)} %constant_dynamic-slice_fusion.2), channel_id=1, source_target_pairs={{0,8},{32,40},{8,16},{40,48},{16,24},{48,56},{24,0},{56,32},{2,10}... | collective-permute-start | bytes 1179656 | tf_op jit(solution)/shard_map/ppermute | solution.py:37
  259.9 1.6 copy-start.9
  278.4 2.2 copy-start.4
  280.6 4.9 %collective-permute-start.22 = (f32[768,512]{0,1:T(8,128)}, f32[768,512]{0,1:T(8,128)}, u32[]{:S(2)}, u32[]{:S(2)}) collective-permute-start(f32[768,512]{0,1:T(8,128)} %constant_dynamic-slice_fusion.1), channel_id=1, source_target_pairs={{0,32},{32,0},{8,40},{40,8},{16,48},{48,16},{24,56},{56,24},{2,34}... | collective-permute-start | bytes 4718600 | tf_op jit(solution)/shard_map/ppermute | solution.py:37
  281.9 2.0 copy-start.6
  298.0 1.2 copy-start
  299.2 1.2 copy-start.1
  (5 other events, 5.3 us)
Sparse Core Ops, SparseCore 0:
  70.7 180.8 all-gather.1

commit v2 on v1

v2 whole, which is shorter than its diff:
```python
import functools
import jax
import jax.numpy as jnp
from jax import lax
from jax.experimental import pallas as pl
from jax.experimental.pallas import tpu as pltpu
from jax.sharding import PartitionSpec as P

NB = 512
EDGE = 1024
TILE = 128
AXES = ("row", "col")
F32 = jnp.float32
BF16 = jnp.bfloat16
NN = (((1,), (0,)), ((), ()))
NT = (((1,), (1,)), ((), ()))
VMEM = pl.BlockSpec(memory_space=pltpu.VMEM)


def device_index(x, y, z, core):
    return ((x % 2) * 2 + core) * 32 + (z % 4) * 8 + (y % 4) * 2 + (x % 4) // 2


def route(rule):
    pairs = []
    for x in range(4):
        for y in range(4):
            for z in range(4):
                for core in range(2):
                    target = rule(x, y, z, core)
                    if target is not None:
                        pairs.append((device_index(x, y, z, core), device_index(*target)))
    return pairs


def send(value, rule):
    return lax.ppermute(value, AXES, route(rule))


def swap_cores(value):
    return send(value, lambda x, y, z, c: (x, y, z, 1 - c))


def split(value):
    high = value.astype(BF16)
    return high, (value - high.astype(F32)).astype(BF16)


def dot3(a, b, dims=NN):
    ah, al = split(a)
    bh, bl = split(b)
    mul = lambda p, q: lax.dot_general(p, q, dims, preferred_element_type=F32)
    return mul(ah, bh) + (mul(ah, bl) + mul(al, bh))


def dot_full(a, b, dims=NN):
    return lax.dot_general(a, b, dims, precision=lax.Precision.HIGHEST, preferred_element_type=F32)


def factor_tile(work, inverse, factor_t):
    rows = lax.broadcasted_iota(jnp.int32, (TILE, TILE), 0)
    lanes = lax.broadcasted_iota(jnp.int32, (TILE, TILE), 1)
    inverse[...] = jnp.where(rows == lanes, F32(1), F32(0))
    lane8 = lax.broadcasted_iota(jnp.int32, (8, TILE), 1)

    def group(g, carry):
        top = work[0:8, :]
        cols = [jnp.broadcast_to(top[:, s : s + 1], (8, TILE)) for s in range(8)]
        e = [[cols[s][t : t + 1, :] if s <= t else None for s in range(8)] for t in range(8)]
        low = [[None] * 8 for _ in range(8)]
        scale = [None] * 8
        for s in range(8):
            r = lax.rsqrt(e[s][s])
            r = r * (F32(1.5) - F32(0.5) * e[s][s] * r * r)
            scale[s] = r
            for t in range(s + 1, 8):
                low[t][s] = e[t][s] * r
            for u in range(s + 1, 8):
                for t in range(u, 8):
                    e[t][u] = e[t][u] - low[t][s] * low[u][s]
        inv = [[None] * 8 for _ in range(8)]
        for s in range(8):
            inv[s][s] = scale[s]
            for t in range(s + 1, 8):
                total = low[t][s] * inv[s][s]
                for u in range(s + 1, t):
                    total = total + low[t][u] * inv[u][s]
                inv[t][s] = -total * scale[t]
        zero = jnp.zeros((1, TILE), F32)
        eye = inverse[pl.ds(pl.multiple_of(g * 8, 8), 8), :]
        upper = None
        solved = None
        for t in range(8):
            column = jnp.concatenate([inv[s][t] if s >= t else zero for s in range(8)], axis=0)
            a = column * top[t : t + 1, :]
            b = column * eye[t : t + 1, :]
            upper = a if upper is None else upper + a
            solved = b if solved is None else solved + b
        upper = jnp.where(lane8 < TILE - 8 * g, upper, F32(0))
        factor_t[pl.ds(pl.multiple_of(g * 8, 8), 8), :] = pltpu.roll(upper, 8 * g, 1)
        side = upper.T
        for q in range(1, 16):
            at = pl.ds(pl.multiple_of(((g + q) % 16) * 8, 8), 8)
            new = work[8 * q : 8 * q + 8, :]
            row = inverse[at, :]
            for s in range(8):
                mult = jnp.broadcast_to(side[8 * q : 8 * q + 8, s : s + 1], (8, TILE))
                new = new - mult * upper[s : s + 1, :]
                row = row - mult * solved[s : s + 1, :]
            work[8 * q - 8 : 8 * q, :] = pltpu.roll(new, TILE - 8, 1)
            inverse[at, :] = row
        inverse[pl.ds(pl.multiple_of(g * 8, 8), 8), :] = solved
        return carry

    lax.fori_loop(0, 16, group, 0)


def factor_blocks(blocks, mat, low, inv, inv_t, work, tile_inv, tile_t):
    rows = lax.broadcasted_iota(jnp.int32, (TILE, TILE), 0)
    lanes = lax.broadcasted_iota(jnp.int32, (TILE, TILE), 1)
    for b in blocks:
        s, e = b * TILE, (b + 1) * TILE
        work[...] = mat[s:e, s:e]
        factor_tile(work, tile_inv, tile_t)
        x = jnp.where(rows >= lanes, tile_inv[...], F32(0))
        low[s:e, s:e] = jnp.where(rows >= lanes, tile_t[...].T, F32(0))
        inv[s:e, s:e] = x
        inv_t[s:e, s:e] = x.T
        if b > 0:
            left = dot_full(low[s:e, 0:s], inv[0:s, 0:s])
            left = -dot_full(x, left)
            inv[s:e, 0:s] = left
            inv_t[0:s, s:e] = left.T
        if e < NB:
            panel = dot_full(mat[e:NB, s:e], x, NT)
            low[e:NB, s:e] = panel
            for c in range(e, NB, 2 * TILE):
                d = min(c + 2 * TILE, NB)
                mat[c:NB, c:d] = mat[c:NB, c:d] - dot_full(panel[c - e :], panel[c - e : d - e], NT)


def open_kernel(source, mat, low, inv, inv_t, work, tile_inv, tile_t):
    mat[...] = source[...]
    low[...] = jnp.zeros_like(low)
    inv[...] = jnp.zeros_like(inv)
    inv_t[...] = jnp.zeros_like(inv_t)
    factor_blocks((0, 1), mat, low, inv, inv_t, work, tile_inv, tile_t)


def carry_on(sources, mat, low, inv, inv_t, tiles):
    for source, target in zip(sources, (mat, low, inv, inv_t)):
        target[...] = source[...]
    factor_blocks((2, 3), mat, low, inv, inv_t, *tiles)


def close_kernel(m, l, i, t, low, inv, inv_t, mat, *tiles):
    carry_on((m, l, i, t), mat, low, inv, inv_t, tiles)


def below_kernel(m, l, i, t, a10, a11, low, inv, inv_t, below, below_t, rest, mat, *tiles):
    carry_on((m, l, i, t), mat, low, inv, inv_t, tiles)
    panel = dot_full(a10[...], inv_t[...])
    below[...] = panel
    below_t[...] = panel.T
    rest[...] = a11[...] - dot_full(panel, panel, NT)


def squares(kernel, name, outs, held, *args):
    return pl.pallas_call(
        kernel,
        out_shape=(jax.ShapeDtypeStruct((NB, NB), F32),) * outs,
        in_specs=[VMEM] * len(args),
        out_specs=(VMEM,) * outs,
        scratch_shapes=[pltpu.VMEM((NB, NB), F32)] * held + [pltpu.VMEM((TILE, TILE), F32)] * 3,
        compiler_params=pltpu.CompilerParams(vmem_limit_bytes=24 << 20),
        cost_estimate=pl.CostEstimate(flops=30_000_000_000, bytes_accessed=len(args) << 20, transcendentals=0),
        name=name,
    )(*args)


def factor_all(a00, a10, a11):
    state = squares(open_kernel, "open", 4, 0, a00)
    l0, x0, _, l10, _, rest = squares(below_kernel, "below", 6, 1, *state, a10, a11)
    state = squares(open_kernel, "open", 4, 0, rest)
    l1, x1, _ = squares(close_kernel, "close", 3, 1, *state)
    zero = jnp.zeros_like(l0)
    x10 = -jnp.dot(x1, jnp.dot(l10, x0, precision="highest"), precision="highest")
    return jnp.block([[l0, zero], [l10, l1]]), jnp.block([[x0, zero], [x10, x1]])


def solve_kernel(col_ref, g0, g1, inv0, inv0_t, below, below_t, inv1, inv1_t, wh, wl, y, mid):
    col = col_ref[0]
    half = NB // 2
    y0 = jnp.concatenate([dot3(inv0[0:half, 0:half], g0[0:half, :]), dot3(inv0[half:, :], g0[...])], axis=0)
    rest = g1[...] - dot3(below[...], y0)
    y1 = jnp.concatenate([dot3(inv1[0:half, 0:half], rest[0:half, :]), dot3(inv1[half:, :], rest)], axis=0)
    rows = lax.broadcasted_iota(jnp.int32, (NB, NB), 0)
    lanes = lax.broadcasted_iota(jnp.int32, (NB, NB), 1)
    y[0:NB, :] = y0[:, NB:]
    y[NB:, :] = y1[:, NB:]
    unit = jnp.where(rows == lanes, F32(-1), F32(0))
    mid[0:NB, NB:] = y0[:, NB:]
    mid[NB:, NB:] = y1[:, NB:]
    mid[0:NB, 0:NB] = jnp.where(col == 0, unit, jnp.where(col == 1, F32(0), y0[:, 0:NB]))
    mid[NB:, 0:NB] = jnp.where(col == 1, unit, jnp.where(col == 0, F32(0), y1[:, 0:NB]))
    w1 = jnp.concatenate(
        [dot3(inv1_t[0:half, :], mid[NB:, :]), dot3(inv1_t[half:, half:], mid[NB + half :, :])], axis=0
    )
    h, l = split(w1)
    wh[NB:, :] = h
    wl[NB:, :] = l
    z0 = mid[0:NB, :] - dot3(below_t[...], w1)
    w0 = jnp.concatenate([dot3(inv0_t[0:half, :], z0), dot3(inv0_t[half:, half:], z0[half:, :])], axis=0)
    h, l = split(w0)
    wh[0:NB, :] = h
    wl[0:NB, :] = l


def update_kernel(place, wh, wl, special, y, *refs):
    a_refs, b_refs = refs[0:5], refs[5:10]
    mat, rhs, out, out_rhs, rbuf, mbuf, vbuf, obuf, qbuf, rsem, msem, vsem, osem, qsem = refs[10:]
    row, col, here_z, here_y = place[0], place[1], place[2], place[3]
    steps = 8

    def chunk(s, k):
        z = (here_z + jnp.where(s < 4, s, k)) % 4
        v = (here_y + jnp.where(s < 4, k, s - 4)) % 4
        return pl.multiple_of((z * 4 + v) * 2 * TILE + jnp.where(s < 4, 0, TILE), TILE)

    def load(s, slot):
        for t in range(steps):
            refs5 = a_refs if t < 4 else b_refs
            own, plus, minus, far0, far1 = refs5

            @pl.when(s == t)
            def _(t=t, own=own, plus=plus, minus=minus, far0=far0, far1=far1):
                if t % 4 == 2:
                    pltpu.make_async_copy(far0, rbuf.at[slot, pl.ds(0, NB // 2)], rsem.at[slot]).start()
                    pltpu.make_async_copy(far1, rbuf.at[slot, pl.ds(NB // 2, NB // 2)], rsem.at[slot]).start()
                else:
                    pltpu.make_async_copy((own, plus, None, minus)[t % 4], rbuf.at[slot], rsem.at[slot]).start()

        for k in range(4):
            at = chunk(s, k)
            pltpu.make_async_copy(mat.at[pl.ds(at, TILE)], mbuf.at[slot, pl.ds(k * TILE, TILE)], msem.at[slot]).start()
            pltpu.make_async_copy(rhs.at[pl.ds(at, TILE)], vbuf.at[slot, pl.ds(k * TILE, TILE)], vsem.at[slot]).start()

    def drain(slot):
        pltpu.make_async_copy(obuf.at[slot], obuf.at[slot], osem.at[slot]).wait()
        pltpu.make_async_copy(qbuf.at[slot], qbuf.at[slot], qsem.at[slot]).wait()

    mul = lambda p, q: lax.dot_general(p, q, NN, preferred_element_type=F32)
    load(0, 0)

    def step(s, carry):
        slot = s % 2

        @pl.when(s + 1 < steps)
        def _():
            load(s + 1, 1 - slot)

        pltpu.make_async_copy(rbuf.at[slot], rbuf.at[slot], rsem.at[slot]).wait()
        pltpu.make_async_copy(mbuf.at[slot], mbuf.at[slot], msem.at[slot]).wait()
        pltpu.make_async_copy(vbuf.at[slot], vbuf.at[slot], vsem.at[slot]).wait()

        @pl.when(s >= 2)
        def _():
            drain(slot)

        rh, rl = split(rbuf[slot])
        acc = mul(rh, wh[...]) + (mul(rh, wl[...]) + mul(rl, wh[...]))
        obuf[slot] = jnp.where(col < 2, F32(0), mbuf[slot]) - acc[:, 0:NB]
        qbuf[slot] = vbuf[slot] - acc[:, NB:]
        for k in range(4):
            at = chunk(s, k)

            @pl.when(jnp.logical_and(row < 2, at < NB))
            def _():
                obuf[slot, pl.ds(k * TILE, TILE), :] = special[pl.ds(pl.multiple_of(at % NB, TILE), TILE), :]
                qbuf[slot, pl.ds(k * TILE, TILE), :] = y[pl.ds(pl.multiple_of(at % NB, TILE), TILE), :]

            pltpu.make_async_copy(obuf.at[slot, pl.ds(k * TILE, TILE)], out.at[pl.ds(at, TILE)], osem.at[slot]).start()
            pltpu.make_async_copy(
                qbuf.at[slot, pl.ds(k * TILE, TILE)], out_rhs.at[pl.ds(at, TILE)], qsem.at[slot]
            ).start()
        return carry

    lax.fori_loop(0, steps, step, 0)
    drain(0)
    drain(1)


def ordered(parts, first):
    both = jnp.concatenate(parts + parts, axis=0)
    size = parts[0].shape[0]
    return lax.dynamic_slice_in_dim(both, (4 - first) % 4 * size, 4 * size, 0)


def turn_kernel(source, target):
    target[...] = source[...].T


def turn(value):
    return pl.pallas_call(
        turn_kernel,
        out_shape=jax.ShapeDtypeStruct(value.shape, F32),
        in_specs=[VMEM],
        out_specs=VMEM,
        compiler_params=pltpu.CompilerParams(vmem_limit_bytes=8 << 20),
        cost_estimate=pl.CostEstimate(flops=0, bytes_accessed=2 << 20, transcendentals=0),
        name="turn",
    )(value)


def ring(axis, d):
    if axis == "y":
        return lambda X, Y, Z, C: (X, Y - d, Z, C)
    return lambda X, Y, Z, C: (X, Y, Z - d, C)


def tie(*values):
    return lax.optimization_barrier(values)


def body(matrix, right_sides):
    row = lax.axis_index("row")
    col = lax.axis_index("col")
    core, x_lo = row % 2, row // 2
    z, y, x = col // 8, col // 2 % 4, col % 2 * 2 + row // 2
    first = matrix[0:NB]

    part, half = NB // 4, NB // 2
    turned = turn(first)

    recv = []
    for d in (1, 2, 3):
        block = jnp.where(x == 2, (2 + d) % 4, d)
        recv.append(
            send(
                lax.dynamic_slice_in_dim(first, block * part, part, 0),
                lambda X, Y, Z, C, d=d: (X + d, Y, Z, C) if (Y, Z) == (0, 0) and X % 2 == 0 else None,
            )
        )
    here = lax.dynamic_slice_in_dim(first, x * part, part, 0)
    r1, r2, r3 = recv
    main = jnp.where(x == 0, here, jnp.where(x == 1, r1, jnp.where(x == 2, r2, r3)))
    corner = jnp.where(x == 0, r2, jnp.where(x == 1, r3, jnp.where(x == 2, here, r1)))
    held, turned = tie(jnp.concatenate([main, corner], axis=0), turned)

    def strew(m):
        def rule(X, Y, Z, C):
            if X % 2:
                return None
            u, v = m // 2 ^ C, m % 2 ^ C
            return (2 * (X // 2 ^ v) + Y % 2, Y // 2 * 2 + (Y % 2 ^ u), Z, X // 2)

        h = jnp.bitwise_xor(jnp.bitwise_xor(y % 2, m // 2), core)
        return send(lax.dynamic_slice_in_dim(turned, h * half, half, 0), rule)

    small = held.shape[0] // 4
    mine = jnp.where(z == 0, held[0:small], F32(0))
    for d in (1, 2, 3):
        mine = mine + send(
            held[d * small : (d + 1) * small], lambda X, Y, Z, C, d=d: (X, Y, d, C) if (Y, Z) == (0, 0) else None
        )
    got = [strew(0), strew(1)]
    mine, turned, *got = tie(mine, turned, *got)

    every = jnp.where(y == 0, mine, F32(0))
    for d in (1, 2, 3):
        every = every + send(mine, lambda X, Y, Z, C, d=d: (X, d, Z, C) if Y == 0 else None)
    got += [strew(2), strew(3)]
    every, *got = tie(every, *got)

    zs = [every] + [send(every, ring("z", d)) for d in (1, 2, 3)]
    u = jnp.bitwise_xor(y % 2, x % 2)
    v = jnp.bitwise_xor(x // 2, core)
    pick = lambda a, b, p: jnp.where(a == 0, jnp.where(b == 0, p[0], p[1]), jnp.where(b == 0, p[2], p[3]))
    piece = jnp.concatenate([pick(u, v, got), pick(1 - u, 1 - v, got)], axis=1)
    piece_a, piece_b = piece[0:TILE], piece[TILE:]
    a1, a3 = send(piece_a, ring("y", 1)), send(piece_a, ring("y", 3))
    ring_z = ordered(zs, z)
    ring_z, piece_a, piece_b, a1, a3 = tie(ring_z, piece_a, piece_b, a1, a3)

    mains = [ring_z[0:part]] + [send(ring_z[0:part], lambda X, Y, Z, C, d=d: (X - d, Y, Z, C)) for d in (1, 2, 3)]
    a2, b1 = send(piece_a, ring("y", 2)), send(piece_b, ring("z", 1))
    main = ordered(mains, x)
    main, a2, b1, piece_b = tie(main, a2, b1, piece_b)
    other_main = swap_cores(main)
    b3, b2 = send(piece_b, ring("z", 3)), send(piece_b, ring("z", 2))
    a00 = jnp.where(core == 0, main, other_main)
    a10 = jnp.where(core == 0, other_main, main)
    tail = ring_z[part:]
    a00, tail = tie(a00, tail)
    corners = [tail] + [send(tail, lambda X, Y, Z, C, d=d: (X - d, Y, Z, C)) for d in (1, 2, 3)]

    state = squares(open_kernel, "open0", 4, 0, a00)

    state, b2, b3, corners = tie(state, b2, b3, corners)
    corner = ordered(corners, x)
    other_corner = swap_cores(corner)
    a11 = jnp.where(core == 0, other_corner, corner)
    rows_a = jnp.concatenate([piece_a, a1, a2, a3], axis=0)
    rows_b = jnp.concatenate([piece_b, b1, b2, b3], axis=0)
    fars = []
    for rows, axis in ((rows_a, "z"), (rows_b, "y")):
        fars.append((send(rows, ring(axis, 1)), send(rows, ring(axis, 3))))
    first_rows, top_rhs, a11 = tie(first, right_sides[0:NB], a11)

    top = jnp.concatenate([first_rows, top_rhs], axis=1)
    crossed = send(top, lambda X, Y, Z, C: (X + 1, Y, Z, C) if X % 2 == 0 else None)
    l0, inv0, inv0_t, below, below_t, rest = squares(below_kernel, "below0", 6, 1, *state, a10, a11)
    state = squares(open_kernel, "open1", 4, 0, rest)

    state, fars, crossed = tie(state, fars, crossed)
    own = jnp.where(x_lo == 0, top, crossed)
    partner = swap_cores(own)
    gathered = []
    for (plus, minus), rows, axis in ((fars[0], rows_a, "z"), (fars[1], rows_b, "y")):
        far0 = send(plus[0:half], ring(axis, 1))
        far1 = send(minus[half:], ring(axis, 3))
        gathered += [rows, plus, minus, far0, far1]

    l1, inv1, inv1_t = squares(close_kernel, "close1", 3, 1, *state)
    g0 = jnp.where(core == 0, own, partner)
    g1 = jnp.where(core == 0, partner, own)

    width = NB + right_sides.shape[1]
    wh, wl, answer = pl.pallas_call(
        solve_kernel,
        out_shape=(
            jax.ShapeDtypeStruct((EDGE, width), BF16),
            jax.ShapeDtypeStruct((EDGE, width), BF16),
            jax.ShapeDtypeStruct((EDGE, width - NB), F32),
        ),
        in_specs=[pl.BlockSpec(memory_space=pltpu.SMEM)] + [VMEM] * 8,
        out_specs=(VMEM,) * 3,
        scratch_shapes=[pltpu.VMEM((EDGE, width), F32)],
        compiler_params=pltpu.CompilerParams(vmem_limit_bytes=48 << 20),
        cost_estimate=pl.CostEstimate(flops=10_000_000_000, bytes_accessed=16 << 20, transcendentals=0),
        name="solve",
    )(col.reshape(1), g0, g1, inv0, inv0_t, below, below_t, inv1, inv1_t)

    lower = jnp.where(row == 0, jnp.where(col == 0, l0, F32(0)), jnp.where(col == 0, below, l1))
    special = jnp.where(col < 2, lower, F32(0))
    answer = lax.dynamic_slice_in_dim(answer, row % 2 * NB, NB, 0)

    anywhere = pl.BlockSpec(memory_space=pl.ANY)
    pair = lambda *shape: pltpu.VMEM((2,) + shape, F32)
    return pl.pallas_call(
        update_kernel,
        in_specs=[pl.BlockSpec(memory_space=pltpu.SMEM)] + [VMEM] * 4 + [anywhere] * 12,
        out_specs=(anywhere, anywhere),
        out_shape=(
            jax.ShapeDtypeStruct(matrix.shape, F32),
            jax.ShapeDtypeStruct(right_sides.shape, F32),
        ),
        scratch_shapes=[
            pair(NB, EDGE),
            pair(NB, NB),
            pair(NB, width - NB),
            pair(NB, NB),
            pair(NB, width - NB),
        ]
        + [pltpu.SemaphoreType.DMA((2,))] * 5,
        compiler_params=pltpu.CompilerParams(vmem_limit_bytes=48 << 20),
        cost_estimate=pl.CostEstimate(flops=20_000_000_000, bytes_accessed=44 << 20, transcendentals=0),
        name="update",
    )(jnp.stack([row, col, z, y]), wh, wl, special, answer, *gathered, matrix, right_sides)


def solution(mesh):
    specs = (P("row", "col"), P("row", None))
    return jax.shard_map(body, mesh=mesh, in_specs=specs, out_specs=specs, check_vma=False)
```

time: 462 us -> 279 us (0.60)
  waiting for transfers between devices: 191 us -> 35.3 us
  starting transfers between devices: 59 us -> 80.1 us
  Pallas kernels: 147 us -> 127 us
  between operations: 14.6 us -> 1.97 us
  local copies, waits for them, and re-layouts: 32.7 us -> 21.8 us
  other arithmetic: 15.8 us -> 8.56 us
    ppermute x23 -> x40, waiting for transfers between devices: 191 us -> 35.3 us  [send(): return lax.ppermute(value, AXES, route(rule))]
    ppermute x23 -> x40, starting transfers between devices: 59 us -> 80.1 us  [send(): return lax.ppermute(value, AXES, route(rule))]
    pallas_call x2 -> x6, Pallas kernels: 136 us -> 115 us  [the longest x4 87.5 us: squares(): pl.pallas_call(kernel, out_shape=(jax.ShapeDtypeStruct((NB, NB), F32),) *...]
    slice x11 -> x9, local copies, waits for them, and re-layouts: 10.3 us -> 2.7 us  [the longest x1 0.85 us: body(): ring_z[0:part]]
    unnamed x26 -> x78, local copies, waits for them, and re-layouts: 8.11 us -> 14.3 us
  transfers between devices with their start and end apart: 24 -> 40, of which waited for: 16 -> 12; matrix products, arithmetic and copies ran while one was open for 7% -> 7% of each run, Pallas kernels for 26% -> 36%
where the time goes in v2:
time: 279 us; the launch traced here: 274 us
  Pallas kernels  127 us (46%)
  starting transfers between devices  80.1 us (29%)
  waiting for transfers between devices  35.3 us (13%)
  local copies, waits for them, and re-layouts  21.8 us (8%)
  other arithmetic  8.56 us (3%)
    pallas_call x4, Pallas kernels, squares(): pl.pallas_call(kernel, out_shape=(jax.ShapeDtypeStruct((NB, NB), F32),) *...  87.5 us
    ppermute x40, starting transfers between devices, send(): return lax.ppermute(value, AXES, route(rule))  80.1 us
    ppermute x40, waiting for transfers between devices, send(): return lax.ppermute(value, AXES, route(rule))  35.3 us
    pallas_call x1, Pallas kernels, body(): pl.pallas_call(update_kernel, in_specs=[pl.BlockSpec(memory_space=pltpu.S...  27.5 us
    unnamed x78, local copies, waits for them, and re-layouts  14.3 us
    pallas_call x1, Pallas kernels, body(): pl.pallas_call(solve_kernel, out_shape=(jax.ShapeDtypeStruct((EDGE, width...  11.5 us
  transfers between devices with their start and end apart: 40, of which 12 were waited for; matrix products, arithmetic and copies ran while one was open for 7% of the time, Pallas kernels for 36%

profile of v2, /device:TPU:1, one launch (start us, length us, event | category | flops | bytes accessed | tf_op | source)
XLA Modules:
  0.0 274.5 jit_solution(3705206661533163251)
XLA Ops:
  2.0 4.0 %collective-permute-start = (f32[128,512]{1,0:T(8,128)S(1)}, f32[128,512]{1,0:T(8,128)S(1)}, u32[]{:S(2)}, u32[]{:S(2)}) collective-permute-start(f32[128,512]{1,0:T(8,128)S(1)} %get-tuple-element.140), channel_id=1, source_target_pairs={{0,64},{32,96},{1,65},{33,97}} | collective-permute-start | bytes 786440 | tf_op jit(solution)/shard_map/ppermute | solution.py:37
  6.0 2.6 collective-permute-start.2
  8.6 3.1 %collective-permute-start.1 = (f32[128,512]{1,0:T(8,128)S(1)}, f32[128,512]{1,0:T(8,128)}, u32[]{:S(2)}, u32[]{:S(2)}) collective-permute-start(f32[128,512]{1,0:T(8,128)S(1)} %get-tuple-element.142), channel_id=1, source_target_pairs={{0,1},{32,33},{1,0},{33,32}} | collective-permute-start | bytes 786440 | tf_op jit(solution)/shard_map/ppermute | solution.py:37
  13.5 6.6 %collective-permute-done.1 = f32[128,512]{1,0:T(8,128)} collective-permute-done((f32[128,512]{1,0:T(8,128)S(1)}, f32[128,512]{1,0:T(8,128)}, u32[]{:S(2)}, u32[]{:S(2)}) %collective-permute-start.1) | collective-permute-done | bytes 262176 | tf_op jit(solution)/shard_map/ppermute | solution.py:37
  21.3 1.9 collective-permute-start.7
  23.2 2.1 collective-permute-start.6
  28.7 1.9 collective-permute-start.4
  30.9 2.3 collective-permute-done.4
  34.1 4.4 %collective-permute-done.7 = f32[256,512]{1,0:T(8,128)} collective-permute-done((f32[256,512]{1,0:T(8,128)S(1)}, f32[256,512]{1,0:T(8,128)}, u32[]{:S(2)}, u32[]{:S(2)}) %collective-permute-start.7) | collective-permute-done | bytes 524320 | tf_op jit(solution)/shard_map/ppermute | solution.py:37
  39.9 6.2 %collective-permute-start.11 = (f32[256,512]{1,0:T(8,128)S(1)}, f32[256,512]{1,0:T(8,128)S(1)}, u32[]{:S(2)}, u32[]{:S(2)}) collective-permute-start(f32[256,512]{1,0:T(8,128)S(1)} %constant_dynamic-slice_fusion.4), channel_id=1, source_target_pairs={{0,2},{32,1},{8,10},{40,9},{16,18},{48,17},{24,26},{56,25},{2,64},... | collective-permute-start | bytes 1572872 | tf_op jit(solution)/shard_map/ppermute | solution.py:37
  50.1 4.3 %collective-permute-done.9 = f32[64,512]{1,0:T(8,128)S(1)} collective-permute-done((f32[64,512]{1,0:T(8,128)S(1)}, f32[64,512]{1,0:T(8,128)S(1)}, u32[]{:S(2)}, u32[]{:S(2)}) %collective-permute-start.9) | collective-permute-done | bytes 131104 | tf_op jit(solution)/shard_map/ppermute | solution.py:37
  54.4 3.6 %collective-permute-done.8 = f32[64,512]{1,0:T(8,128)S(1)} collective-permute-done((f32[64,512]{1,0:T(8,128)S(1)}, f32[64,512]{1,0:T(8,128)S(1)}, u32[]{:S(2)}, u32[]{:S(2)}) %collective-permute-start.8) | collective-permute-done | bytes 131104 | tf_op jit(solution)/shard_map/ppermute | solution.py:37
  58.3 2.6 collective-permute-start.13
  63.2 2.2 collective-permute-start.17
  66.1 7.4 %collective-permute-done.17 = f32[128,1024]{1,0:T(8,128)S(1)} collective-permute-done((f32[128,1024]{1,0:T(8,128)S(1)}, f32[128,1024]{1,0:T(8,128)S(1)}, u32[]{:S(2)}, u32[]{:S(2)}) %collective-permute-start.17) | collective-permute-done | bytes 524320 | tf_op jit(solution)/shard_map/ppermute | solution.py:37
  75.0 1.7 collective-permute-start.19
  82.6 2.0 collective-permute-done.20
  90.3 6.7 %collective-permute-start.23 = (f32[512,512]{1,0:T(8,128)S(1)}, f32[512,512]{1,0:T(8,128)}, u32[]{:S(2)}, u32[]{:S(2)}) collective-permute-start(f32[512,512]{1,0:T(8,128)S(1)} %constant_dynamic-slice_fusion.2), channel_id=1, source_target_pairs={{0,32},{32,0},{8,40},{40,8},{16,48},{48,16},{24,56},{56,24},{2,34}... | collective-permute-start | bytes 3145736 | tf_op jit(solution)/shard_map/ppermute | solution.py:37
  97.6 1.8 collective-permute-start.24
  101.1 2.6 collective-permute-start.27
  104.6 20.9 %open0.1 = (f32[512,512]{1,0:T(8,128)S(1)}, f32[512,512]{1,0:T(8,128)S(1)}, f32[512,512]{1,0:T(8,128)S(1)}, f32[512,512]{1,0:T(8,128)S(1)}) custom-call(f32[512,512]{1,0:T(8,128)S(1)} %get-tuple-element.81.source), custom_call_target="tpu_custom_call" | custom-call | flops 30000001024 | bytes 1048576 | tf_op jit(solution)/shard_map/open0/pallas_call | solution.py:169
  138.6 1.9 collective-permute-start.32
  140.9 2.8 %collective-permute-start.34 = (f32[512,768]{1,0:T(8,128)S(1)}, f32[512,768]{1,0:T(8,128)S(1)}, u32[]{:S(2)}, u32[]{:S(2)}) collective-permute-start(f32[512,768]{1,0:T(8,128)S(1)} %constant_dynamic-update-slice_fusion.24), channel_id=1, source_target_pairs={{0,64},{32,96},{8,72},{40,104},{16,80},{48,112},{24,88},{56,120},{... | collective-permute-start | bytes 4718600 | tf_op jit(solution)/shard_map/ppermute | solution.py:37
  143.7 24.6 %below0.1 = (f32[512,512]{1,0:T(8,128)S(1)}, f32[512,512]{1,0:T(8,128)S(1)}, f32[512,512]{1,0:T(8,128)S(1)}, f32[512,512]{1,0:T(8,128)S(1)}, f32[512,512]{1,0:T(8,128)S(1)}, /*index=5*/f32[512,512]{1,0:T(8,128)S(1)}) custom-call(f32[512,512]{1,0:T(8,128)S(1)} %get-tuple-element.94.m, f32[512,512]{1,0:T(8,128)S(1)} %copy-done.3, f32[512,512]{1,0:T(8,128)S(1)} %copy-done.5, ...), custom_call_target="tpu_custom_call" | custom-call | flops 30000001024 | bytes 6291456 | tf_op jit(solution)/shard_map/below0/pallas_call | solution.py:169
  168.3 20.9 %open1.1 = (f32[512,512]{1,0:T(8,128)S(1)}, f32[512,512]{1,0:T(8,128)S(1)}, f32[512,512]{1,0:T(8,128)S(1)}, f32[512,512]{1,0:T(8,128)S(1)}) custom-call(f32[512,512]{1,0:T(8,128)S(1)} %get-tuple-element.99.source), custom_call_target="tpu_custom_call" | custom-call | flops 30000001024 | bytes 1048576 | tf_op jit(solution)/shard_map/open1/pallas_call | solution.py:169
  192.1 11.9 %collective-permute-start.38 = (f32[256,1024]{1,0:T(8,128)S(1)}, f32[256,1024]{1,0:T(8,128)S(1)}, u32[]{:S(2)}, u32[]{:S(2)}) collective-permute-start(f32[256,1024]{1,0:T(8,128)S(1)} %slice.57), channel_id=1, source_target_pairs={{0,6},{32,38},{8,14},{40,46},{16,22},{48,54},{24,30},{56,62},{2,0}... | collective-permute-start | bytes 3145736 | tf_op jit(solution)/shard_map/ppermute | solution.py:37
  204.0 2.7 collective-permute-start.36
  206.9 4.1 %collective-permute-start.35 = (f32[512,768]{1,0:T(8,128)S(1)}, f32[512,768]{1,0:T(8,128)S(1)}, u32[]{:S(2)}, u32[]{:S(2)}) collective-permute-start(f32[512,768]{1,0:T(8,128)S(1)} %broadcast_select_fusion), channel_id=1, source_target_pairs={{0,32},{32,0},{8,40},{40,8},{16,48},{48,16},{24,56},{56,24},{2,34}... | collective-permute-start | bytes 4718600 | tf_op jit(solution)/shard_map/ppermute | solution.py:37
  210.9 21.1 %close1.1 = (f32[512,512]{1,0:T(8,128)S(1)}, f32[512,512]{1,0:T(8,128)S(1)}, f32[512,512]{1,0:T(8,128)S(1)}) custom-call(f32[512,512]{1,0:T(8,128)S(1)} %get-tuple-element.115.m, f32[512,512]{1,0:T(8,128)S(1)} %get-tuple-element.116.l, f32[512,512]{1,0:T(8,128)S(1)} %get-tuple-element.117.i, f32[512,512]{1,0:T(8,128)S(1)} %get-tuple-element.118.t), custom_call_target="tpu_custom_call" | custom-call | flops 30000001024 | bytes 4194304 | tf_op jit(solution)/shard_map/close1/pallas_call | solution.py:169
  233.4 1.9 broadcast_select_fusion.1
  235.2 11.5 %solve.1 = (bf16[1024,768]{1,0:T(8,128)(2,1)}, bf16[1024,768]{1,0:T(8,128)(2,1)}, f32[1024,256]{1,0:T(8,128)S(1)}) custom-call(s32[1]{0:T(128)} %bitcast.1.col_ref, f32[512,768]{1,0:T(8,128)} %get-tuple-element.131.g0, f32[512,768]{1,0:T(8,128)} %get-tuple-element.130.g1, f32[512,512]{1,0:T(8,128)S(1)} %get-tuple-element.111.inv0, ...), custom_call_target="tpu_custom_call" | custom-call | flops 10000000000 | bytes 16777216 | tf_op jit(solution)/shard_map/solve/pallas_call | solution.py:429
  246.8 27.5 %update.1 = (f32[4096,512]{1,0:T(8,128)}, f32[4096,256]{1,0:T(8,128)}) custom-call(s32[4]{0:T(128)S(1)} %pad_add_fusion.place, bf16[1024,768]{1,0:T(8,128)(2,1)} %get-tuple-element.121.wh, bf16[1024,768]{1,0:T(8,128)(2,1)} %get-tuple-element.122.wl, f32[512,512]{1,0:T(8,128)S(1)} %select_select_fusion.special, f32[512,256]{1,0:T(8,128)S(1)} %constant_dynamic-slice_fusion.y, ...), custom_call_target="tpu_custom_call" | custom-call | flops 20000000000 | bytes 46137344 | tf_op jit(solution)/shard_map/update/pallas_call | solution.py:450
  (168 shorter events, 50.9 us)
Async XLA Ops:
  2.0 10.1 %collective-permute-start = (f32[128,512]{1,0:T(8,128)S(1)}, f32[128,512]{1,0:T(8,128)S(1)}, u32[]{:S(2)}, u32[]{:S(2)}) collective-permute-start(f32[128,512]{1,0:T(8,128)S(1)} %get-tuple-element.140), channel_id=1, source_target_pairs={{0,64},{32,96},{1,65},{33,97}} | collective-permute-start | bytes 786440 | tf_op jit(solution)/shard_map/ppermute | solution.py:37
  8.6 11.6 %collective-permute-start.1 = (f32[128,512]{1,0:T(8,128)S(1)}, f32[128,512]{1,0:T(8,128)}, u32[]{:S(2)}, u32[]{:S(2)}) collective-permute-start(f32[128,512]{1,0:T(8,128)S(1)} %get-tuple-element.142), channel_id=1, source_target_pairs={{0,1},{32,33},{1,0},{33,32}} | collective-permute-start | bytes 786440 | tf_op jit(solution)/shard_map/ppermute | solution.py:37
  21.3 17.2 %collective-permute-start.7 = (f32[256,512]{1,0:T(8,128)S(1)}, f32[256,512]{1,0:T(8,128)}, u32[]{:S(2)}, u32[]{:S(2)}) collective-permute-start(f32[256,512]{1,0:T(8,128)S(1)} %constant_dynamic-slice_fusion.5), channel_id=1, source_target_pairs={{0,1},{32,2},{8,9},{40,10},{16,17},{48,18},{24,25},{56,26},{2,67},... | collective-permute-start | bytes 1572872 | tf_op jit(solution)/shard_map/ppermute | solution.py:37
  23.2 15.3 %collective-permute-start.6 = (f32[256,512]{1,0:T(8,128)S(1)}, f32[256,512]{1,0:T(8,128)}, u32[]{:S(2)}, u32[]{:S(2)}) collective-permute-start(f32[256,512]{1,0:T(8,128)S(1)} %constant_dynamic-slice_fusion.5), channel_id=1, source_target_pairs={{0,0},{32,3},{8,8},{40,11},{16,16},{48,19},{24,24},{56,27},{2,66},... | collective-permute-start | bytes 1572872 | tf_op jit(solution)/shard_map/ppermute | solution.py:37
  38.5 19.5 %collective-permute-start.12 = (f32[256,512]{1,0:T(8,128)S(1)}, f32[256,512]{1,0:T(8,128)S(1)}, u32[]{:S(2)}, u32[]{:S(2)}) collective-permute-start(f32[256,512]{1,0:T(8,128)S(1)} %constant_dynamic-slice_fusion.4), channel_id=1, source_target_pairs={{0,3},{32,0},{8,11},{40,8},{16,19},{48,16},{24,27},{56,24},{2,65},... | collective-permute-start | bytes 1572872 | tf_op jit(solution)/shard_map/ppermute | solution.py:37
  39.9 18.2 %collective-permute-start.11 = (f32[256,512]{1,0:T(8,128)S(1)}, f32[256,512]{1,0:T(8,128)S(1)}, u32[]{:S(2)}, u32[]{:S(2)}) collective-permute-start(f32[256,512]{1,0:T(8,128)S(1)} %constant_dynamic-slice_fusion.4), channel_id=1, source_target_pairs={{0,2},{32,1},{8,10},{40,9},{16,18},{48,17},{24,26},{56,25},{2,64},... | collective-permute-start | bytes 1572872 | tf_op jit(solution)/shard_map/ppermute | solution.py:37
  48.7 9.3 %collective-permute-start.8 = (f32[64,512]{1,0:T(8,128)S(1)}, f32[64,512]{1,0:T(8,128)S(1)}, u32[]{:S(2)}, u32[]{:S(2)}) collective-permute-start(f32[64,512]{1,0:T(8,128)S(1)} %add_add_fusion.1), channel_id=1, source_target_pairs={{0,2},{32,34},{8,10},{40,42},{16,18},{48,50},{24,26},{56,58},{64,6... | collective-permute-start | bytes 393224 | tf_op jit(solution)/shard_map/ppermute | solution.py:37
  58.1 7.8 %collective-permute-start.15 = (f32[64,512]{1,0:T(8,128)S(1)}, f32[64,512]{1,0:T(8,128)S(1)}, u32[]{:S(2)}, u32[]{:S(2)}) collective-permute-start(f32[64,512]{1,0:T(8,128)S(1)} %add_add_fusion), channel_id=1, source_target_pairs={{0,8},{32,40},{8,16},{40,48},{16,24},{48,56},{24,0},{56,32},{2,10}... | collective-permute-start | bytes 393224 | tf_op jit(solution)/shard_map/ppermute | solution.py:37
  58.2 7.7 %collective-permute-start.14 = (f32[64,512]{1,0:T(8,128)S(1)}, f32[64,512]{1,0:T(8,128)S(1)}, u32[]{:S(2)}, u32[]{:S(2)}) collective-permute-start(f32[64,512]{1,0:T(8,128)S(1)} %add_add_fusion), channel_id=1, source_target_pairs={{0,16},{32,48},{8,24},{40,56},{16,0},{48,32},{24,8},{56,40},{2,18}... | collective-permute-start | bytes 393224 | tf_op jit(solution)/shard_map/ppermute | solution.py:37
  58.3 7.6 %collective-permute-start.13 = (f32[64,512]{1,0:T(8,128)S(1)}, f32[64,512]{1,0:T(8,128)S(1)}, u32[]{:S(2)}, u32[]{:S(2)}) collective-permute-start(f32[64,512]{1,0:T(8,128)S(1)} %add_add_fusion), channel_id=1, source_target_pairs={{0,24},{32,56},{8,0},{40,32},{16,8},{48,40},{24,16},{56,48},{2,26}... | collective-permute-start | bytes 393224 | tf_op jit(solution)/shard_map/ppermute | solution.py:37
  63.2 10.3 %collective-permute-start.17 = (f32[128,1024]{1,0:T(8,128)S(1)}, f32[128,1024]{1,0:T(8,128)S(1)}, u32[]{:S(2)}, u32[]{:S(2)}) collective-permute-start(f32[128,1024]{1,0:T(8,128)S(1)} %get-tuple-element.78), channel_id=1, source_target_pairs={{0,2},{32,34},{8,10},{40,42},{16,18},{48,50},{24,26},{56,58},{2,4}... | collective-permute-start | bytes 1572872 | tf_op jit(solution)/shard_map/ppermute | solution.py:37
  65.4 8.8 %collective-permute-start.16 = (f32[128,1024]{1,0:T(8,128)S(1)}, f32[128,1024]{1,0:T(8,128)S(1)}, u32[]{:S(2)}, u32[]{:S(2)}) collective-permute-start(f32[128,1024]{1,0:T(8,128)S(1)} %get-tuple-element.78), channel_id=1, source_target_pairs={{0,6},{32,38},{8,14},{40,46},{16,22},{48,54},{24,30},{56,62},{2,0}... | collective-permute-start | bytes 1572872 | tf_op jit(solution)/shard_map/ppermute | solution.py:37
  76.7 7.8 %collective-permute-start.20 = (f32[128,512]{1,0:T(8,128)S(1)}, f32[128,512]{1,0:T(8,128)S(1)}, u32[]{:S(2)}, u32[]{:S(2)}) collective-permute-start(f32[128,512]{1,0:T(8,128)S(1)} %get-tuple-element.145), channel_id=1, source_target_pairs={{0,64},{32,96},{8,72},{40,104},{16,80},{48,112},{24,88},{56,120},{... | collective-permute-start | bytes 786440 | tf_op jit(solution)/shard_map/ppermute | solution.py:37
  77.6 11.9 %collective-permute-start.21 = (f32[128,1024]{1,0:T(8,128)S(1)}, f32[128,1024]{1,0:T(8,128)S(1)}, u32[]{:S(2)}, u32[]{:S(2)}) collective-permute-start(f32[128,1024]{1,0:T(8,128)S(1)} %get-tuple-element.78), channel_id=1, source_target_pairs={{0,4},{32,36},{8,12},{40,44},{16,20},{48,52},{24,28},{56,60},{2,6}... | collective-permute-start | bytes 1572872 | tf_op jit(solution)/shard_map/ppermute | solution.py:37
  78.4 11.9 %collective-permute-start.22 = (f32[128,1024]{1,0:T(8,128)}, f32[128,1024]{1,0:T(8,128)}, u32[]{:S(2)}, u32[]{:S(2)}) collective-permute-start(f32[128,1024]{1,0:T(8,128)} %get-tuple-element.86), channel_id=1, source_target_pairs={{0,24},{32,56},{8,0},{40,32},{16,8},{48,40},{24,16},{56,48},{2,26}... | collective-permute-start | bytes 1572872 | tf_op jit(solution)/shard_map/ppermute | solution.py:37
  90.3 9.1 %collective-permute-start.23 = (f32[512,512]{1,0:T(8,128)S(1)}, f32[512,512]{1,0:T(8,128)}, u32[]{:S(2)}, u32[]{:S(2)}) collective-permute-start(f32[512,512]{1,0:T(8,128)S(1)} %constant_dynamic-slice_fusion.2), channel_id=1, source_target_pairs={{0,32},{32,0},{8,40},{40,8},{16,48},{48,16},{24,56},{56,24},{2,34}... | collective-permute-start | bytes 3145736 | tf_op jit(solution)/shard_map/ppermute | solution.py:37
  97.0 28.5 %collective-permute-start.25 = (f32[128,1024]{1,0:T(8,128)}, f32[128,1024]{1,0:T(8,128)S(1)}, u32[]{:S(2)}, u32[]{:S(2)}) collective-permute-start(f32[128,1024]{1,0:T(8,128)} %get-tuple-element.86), channel_id=1, source_target_pairs={{0,8},{32,40},{8,16},{40,48},{16,24},{48,56},{24,0},{56,32},{2,10}... | collective-permute-start | bytes 1572872 | tf_op jit(solution)/shard_map/ppermute | solution.py:37
  97.6 28.0 %collective-permute-start.24 = (f32[128,1024]{1,0:T(8,128)}, f32[128,1024]{1,0:T(8,128)S(1)}, u32[]{:S(2)}, u32[]{:S(2)}) collective-permute-start(f32[128,1024]{1,0:T(8,128)} %get-tuple-element.86), channel_id=1, source_target_pairs={{0,16},{32,48},{8,24},{40,56},{16,0},{48,32},{24,8},{56,40},{2,18}... | collective-permute-start | bytes 1572872 | tf_op jit(solution)/shard_map/ppermute | solution.py:37
  100.9 24.7 %collective-permute-start.28 = (f32[128,512]{1,0:T(8,128)S(1)}, f32[128,512]{1,0:T(8,128)S(1)}, u32[]{:S(2)}, u32[]{:S(2)}) collective-permute-start(f32[128,512]{1,0:T(8,128)S(1)} %get-tuple-element.88), channel_id=1, source_target_pairs={{0,64},{32,96},{8,72},{40,104},{16,80},{48,112},{24,88},{56,120},{... | collective-permute-start | bytes 786440 | tf_op jit(solution)/shard_map/ppermute | solution.py:37
  101.1 24.4 %collective-permute-start.27 = (f32[128,512]{1,0:T(8,128)S(1)}, f32[128,512]{1,0:T(8,128)S(1)}, u32[]{:S(2)}, u32[]{:S(2)}) collective-permute-start(f32[128,512]{1,0:T(8,128)S(1)} %get-tuple-element.88), channel_id=1, source_target_pairs={{0,1},{32,33},{8,9},{40,41},{16,17},{48,49},{24,25},{56,57},{2,3},... | collective-permute-start | bytes 786440 | tf_op jit(solution)/shard_map/ppermute | solution.py:37
  103.7 21.8 %collective-permute-start.26 = (f32[128,512]{1,0:T(8,128)S(1)}, f32[128,512]{1,0:T(8,128)S(1)}, u32[]{:S(2)}, u32[]{:S(2)}) collective-permute-start(f32[128,512]{1,0:T(8,128)S(1)} %get-tuple-element.88), channel_id=1, source_target_pairs={{0,65},{32,97},{8,73},{40,105},{16,81},{48,113},{24,89},{56,121},{... | collective-permute-start | bytes 786440 | tf_op jit(solution)/shard_map/ppermute | solution.py:37
  128.7 11.8 %collective-permute-start.29 = (f32[512,512]{1,0:T(8,128)}, f32[512,512]{1,0:T(8,128)}, u32[]{:S(2)}, u32[]{:S(2)}) collective-permute-start(f32[512,512]{1,0:T(8,128)} %constant_dynamic-slice_fusion.1), channel_id=1, source_target_pairs={{0,32},{32,0},{8,40},{40,8},{16,48},{48,16},{24,56},{56,24},{2,34}... | collective-permute-start | bytes 3145736 | tf_op jit(solution)/shard_map/ppermute | solution.py:37
  132.7 56.5 %collective-permute-start.31 = (f32[512,1024]{1,0:T(8,128)S(1)}, f32[512,1024]{1,0:T(8,128)S(1)}, u32[]{:S(2)}, u32[]{:S(2)}) collective-permute-start(f32[512,1024]{1,0:T(8,128)S(1)} %constant_dynamic-update-slice_fusion.26.refs_0_), channel_id=1, source_target_pairs={{0,8},{32,40},{8,16},{40,48},{16,24},{48,56},{24,0},{56,32},{2,10}... | collective-permute-start | bytes 6291464 | tf_op jit(solution)/shard_map/ppermute | solution.py:37
  133.7 55.4 %collective-permute-start.30 = (f32[512,1024]{1,0:T(8,128)S(1)}, f32[512,1024]{1,0:T(8,128)S(1)}, u32[]{:S(2)}, u32[]{:S(2)}) collective-permute-start(f32[512,1024]{1,0:T(8,128)S(1)} %constant_dynamic-update-slice_fusion.26.refs_0_), channel_id=1, source_target_pairs={{0,24},{32,56},{8,0},{40,32},{16,8},{48,40},{24,16},{56,48},{2,26}... | collective-permute-start | bytes 6291464 | tf_op jit(solution)/shard_map/ppermute | solution.py:37
  137.7 51.5 %collective-permute-start.33 = (f32[512,1024]{1,0:T(8,128)S(1)}, f32[512,1024]{1,0:T(8,128)S(1)}, u32[]{:S(2)}, u32[]{:S(2)}) collective-permute-start(f32[512,1024]{1,0:T(8,128)S(1)} %constant_dynamic-update-slice_fusion.30.refs_5_), channel_id=1, source_target_pairs={{0,2},{32,34},{8,10},{40,42},{16,18},{48,50},{24,26},{56,58},{2,4}... | collective-permute-start | bytes 6291464 | tf_op jit(solution)/shard_map/ppermute | solution.py:37
  138.6 50.7 %collective-permute-start.32 = (f32[512,1024]{1,0:T(8,128)S(1)}, f32[512,1024]{1,0:T(8,128)S(1)}, u32[]{:S(2)}, u32[]{:S(2)}) collective-permute-start(f32[512,1024]{1,0:T(8,128)S(1)} %constant_dynamic-update-slice_fusion.30.refs_5_), channel_id=1, source_target_pairs={{0,6},{32,38},{8,14},{40,46},{16,22},{48,54},{24,30},{56,62},{2,0}... | collective-permute-start | bytes 6291464 | tf_op jit(solution)/shard_map/ppermute | solution.py:37
  140.9 48.4 %collective-permute-start.34 = (f32[512,768]{1,0:T(8,128)S(1)}, f32[512,768]{1,0:T(8,128)S(1)}, u32[]{:S(2)}, u32[]{:S(2)}) collective-permute-start(f32[512,768]{1,0:T(8,128)S(1)} %constant_dynamic-update-slice_fusion.24), channel_id=1, source_target_pairs={{0,64},{32,96},{8,72},{40,104},{16,80},{48,112},{24,88},{56,120},{... | collective-permute-start | bytes 4718600 | tf_op jit(solution)/shard_map/ppermute | solution.py:37
  192.0 54.7 %collective-permute-start.39 = (f32[256,1024]{1,0:T(8,128)S(1)}, f32[256,1024]{1,0:T(8,128)S(1)}, u32[]{:S(2)}, u32[]{:S(2)}) collective-permute-start(f32[256,1024]{1,0:T(8,128)S(1)} %slice.58), channel_id=1, source_target_pairs={{0,2},{32,34},{8,10},{40,42},{16,18},{48,50},{24,26},{56,58},{2,4}... | collective-permute-start | bytes 3145736 | tf_op jit(solution)/shard_map/ppermute | solution.py:37
  192.1 54.7 %collective-permute-start.38 = (f32[256,1024]{1,0:T(8,128)S(1)}, f32[256,1024]{1,0:T(8,128)S(1)}, u32[]{:S(2)}, u32[]{:S(2)}) collective-permute-start(f32[256,1024]{1,0:T(8,128)S(1)} %slice.57), channel_id=1, source_target_pairs={{0,6},{32,38},{8,14},{40,46},{16,22},{48,54},{24,30},{56,62},{2,0}... | collective-permute-start | bytes 3145736 | tf_op jit(solution)/shard_map/ppermute | solution.py:37
  204.0 42.8 %collective-permute-start.37 = (f32[256,1024]{1,0:T(8,128)S(1)}, f32[256,1024]{1,0:T(8,128)S(1)}, u32[]{:S(2)}, u32[]{:S(2)}) collective-permute-start(f32[256,1024]{1,0:T(8,128)S(1)} %slice.56), channel_id=1, source_target_pairs={{0,8},{32,40},{8,16},{40,48},{16,24},{48,56},{24,0},{56,32},{2,10}... | collective-permute-start | bytes 3145736 | tf_op jit(solution)/shard_map/ppermute | solution.py:37
  204.0 42.8 %collective-permute-start.36 = (f32[256,1024]{1,0:T(8,128)S(1)}, f32[256,1024]{1,0:T(8,128)S(1)}, u32[]{:S(2)}, u32[]{:S(2)}) collective-permute-start(f32[256,1024]{1,0:T(8,128)S(1)} %slice.55), channel_id=1, source_target_pairs={{0,24},{32,56},{8,0},{40,32},{16,8},{48,40},{24,16},{56,48},{2,26}... | collective-permute-start | bytes 3145736 | tf_op jit(solution)/shard_map/ppermute | solution.py:37
  206.9 26.5 %collective-permute-start.35 = (f32[512,768]{1,0:T(8,128)S(1)}, f32[512,768]{1,0:T(8,128)S(1)}, u32[]{:S(2)}, u32[]{:S(2)}) collective-permute-start(f32[512,768]{1,0:T(8,128)S(1)} %broadcast_select_fusion), channel_id=1, source_target_pairs={{0,32},{32,0},{8,40},{40,8},{16,48},{48,16},{24,56},{56,24},{2,34}... | collective-permute-start | bytes 4718600 | tf_op jit(solution)/shard_map/ppermute | solution.py:37
  (35 other events, 145.1 us)

commit v3 on v2

--- a/solution.py
+++ b/solution.py
@@ -62,17 +62,17 @@
     lanes = lax.broadcasted_iota(jnp.int32, (TILE, TILE), 1)
     inverse[...] = jnp.where(rows == lanes, F32(1), F32(0))
     lane8 = lax.broadcasted_iota(jnp.int32, (8, TILE), 1)
-
-    def group(g, carry):
-        top = work[0:8, :]
-        cols = [jnp.broadcast_to(top[:, s : s + 1], (8, TILE)) for s in range(8)]
-        e = [[cols[s][t : t + 1, :] if s <= t else None for s in range(8)] for t in range(8)]
+    row8 = lax.broadcasted_iota(jnp.int32, (8, TILE), 0)
+    spread = lambda v, s: jnp.broadcast_to(v[:, s : s + 1], (8, TILE))
+    tile = lambda g: pl.ds(pl.multiple_of(g % 16 * 8, 8), 8)
+
+    def pivot(g, top, cols, eye, below, below_eye):
+        whole = lambda v, t: jnp.broadcast_to(v[t : t + 1, :], (8, TILE))
+        e = [[whole(cols[s], t) if s <= t else None for s in range(8)] for t in range(8)]
         low = [[None] * 8 for _ in range(8)]
         scale = [None] * 8
         for s in range(8):
-            r = lax.rsqrt(e[s][s])
-            r = r * (F32(1.5) - F32(0.5) * e[s][s] * r * r)
-            scale[s] = r
+            scale[s] = r = lax.rsqrt(e[s][s])
             for t in range(s + 1, 8):
                 low[t][s] = e[t][s] * r
             for u in range(s + 1, 8):
@@ -86,33 +86,57 @@
                 for u in range(s + 1, t):
                     total = total + low[t][u] * inv[u][s]
                 inv[t][s] = -total * scale[t]
-        zero = jnp.zeros((1, TILE), F32)
-        eye = inverse[pl.ds(pl.multiple_of(g * 8, 8), 8), :]
         upper = None
         solved = None
         for t in range(8):
-            column = jnp.concatenate([inv[s][t] if s >= t else zero for s in range(8)], axis=0)
+            column = jnp.where(row8 == t, inv[t][t], F32(0))
+            for s in range(t + 1, 8):
+                column = jnp.where(row8 == s, inv[s][t], column)
             a = column * top[t : t + 1, :]
             b = column * eye[t : t + 1, :]
             upper = a if upper is None else upper + a
             solved = b if solved is None else solved + b
         upper = jnp.where(lane8 < TILE - 8 * g, upper, F32(0))
-        factor_t[pl.ds(pl.multiple_of(g * 8, 8), 8), :] = pltpu.roll(upper, 8 * g, 1)
-        side = upper.T
-        for q in range(1, 16):
-            at = pl.ds(pl.multiple_of(((g + q) % 16) * 8, 8), 8)
-            new = work[8 * q : 8 * q + 8, :]
-            row = inverse[at, :]
-            for s in range(8):
-                mult = jnp.broadcast_to(side[8 * q : 8 * q + 8, s : s + 1], (8, TILE))
-                new = new - mult * upper[s : s + 1, :]
-                row = row - mult * solved[s : s + 1, :]
+        back = None
+        for s in range(8):
+            column = jnp.where(row8 == s, inv[s][s], F32(0))
+            for t in range(s):
+                column = jnp.where(row8 == t, inv[s][t], column)
+            a = column * upper[s : s + 1, :]
+            b = column * solved[s : s + 1, :]
+            back = (a, b) if back is None else (back[0] + a, back[1] + b)
+        below, below_eye = apply(below, below_eye, back)
+        cols = tuple(spread(below, 8 + s) for s in range(8))
+        return upper, solved, back, pltpu.roll(below, TILE - 8, 1), below_eye, cols
+
+    def apply(new, row, back):
+        mults = [spread(new, s) for s in range(8)]
+        for s in range(8):
+            new = new - mults[s] * back[0][s : s + 1, :]
+            row = row - mults[s] * back[1][s : s + 1, :]
+        return new, row
+
+    def group(last, g, carry):
+        back, top, eye, cols = carry
+        below, below_eye = apply(work[16:24, :], inverse[tile(g + 2), :], back)
+        for q in range(3, last):
+            new, row = apply(work[8 * q : 8 * q + 8, :], inverse[tile(g + q), :], back)
             work[8 * q - 8 : 8 * q, :] = pltpu.roll(new, TILE - 8, 1)
-            inverse[at, :] = row
-        inverse[pl.ds(pl.multiple_of(g * 8, 8), 8), :] = solved
-        return carry
-
-    lax.fori_loop(0, 16, group, 0)
+            inverse[tile(g + q), :] = row
+        work[8 * last - 8 : 8 * last, :] = jnp.zeros((8, TILE), F32)
+        carry = pivot(g + 1, top, cols, eye, pltpu.roll(below, TILE - 8, 1), below_eye)
+        factor_t[tile(g + 1), :] = pltpu.roll(carry[0], 8 * (g + 1), 1)
+        inverse[tile(g + 1), :] = carry[1]
+        return carry[2:]
+
+    top = work[0:8, :]
+    cols = tuple(spread(top, s) for s in range(8))
+    carry = pivot(0, top, cols, inverse[0:8, :], work[8:16, :], inverse[8:16, :])
+    factor_t[0:8, :] = carry[0]
+    inverse[0:8, :] = carry[1]
+    carry = carry[2:]
+    for first, stop, last in ((0, 3, 16), (3, 6, 13), (6, 9, 10), (9, 12, 7), (12, 15, 4)):
+        carry = lax.fori_loop(first, stop, functools.partial(group, last), carry)
 
 
 def factor_blocks(blocks, mat, low, inv, inv_t, work, tile_inv, tile_t):
@@ -139,6 +163,22 @@
                 mat[c:NB, c:d] = mat[c:NB, c:d] - dot_full(panel[c - e :], panel[c - e : d - e], NT)
 
 
+def place_quarters(place, mine, other, target, core):
+    quarter = NB // 4
+    for d in range(4):
+        at = pl.multiple_of((place[0] + d) % 4 * quarter, quarter)
+        rows = slice(d * quarter, (d + 1) * quarter)
+        target[pl.ds(at, quarter), :] = jnp.where(place[1] == core, mine[rows, :], other[rows, :])
+
+
+def first_kernel(place, mine, other, mat, low, inv, inv_t, work, tile_inv, tile_t):
+    place_quarters(place, mine, other, mat, 0)
+    low[...] = jnp.zeros_like(low)
+    inv[...] = jnp.zeros_like(inv)
+    inv_t[...] = jnp.zeros_like(inv_t)
+    factor_blocks((0, 1), mat, low, inv, inv_t, work, tile_inv, tile_t)
+
+
 def open_kernel(source, mat, low, inv, inv_t, work, tile_inv, tile_t):
     mat[...] = source[...]
     low[...] = jnp.zeros_like(low)
@@ -157,39 +197,37 @@
     carry_on((m, l, i, t), mat, low, inv, inv_t, tiles)
 
 
-def below_kernel(m, l, i, t, a10, a11, low, inv, inv_t, below, below_t, rest, mat, *tiles):
+def below_kernel(place, m, l, i, t, mine, other, edge, far_edge, low, inv, inv_t, below, below_t, rest, mat, *tiles):
     carry_on((m, l, i, t), mat, low, inv, inv_t, tiles)
-    panel = dot_full(a10[...], inv_t[...])
+    place_quarters(place, mine, other, rest, 1)
+    panel = dot_full(rest[...], inv_t[...])
     below[...] = panel
     below_t[...] = panel.T
-    rest[...] = a11[...] - dot_full(panel, panel, NT)
-
-
-def squares(kernel, name, outs, held, *args):
+    place_quarters(place, edge, far_edge, rest, 1)
+    rest[...] = rest[...] - dot_full(panel, panel, NT)
+
+
+def squares(kernel, name, outs, held, *args, place=()):
     return pl.pallas_call(
         kernel,
         out_shape=(jax.ShapeDtypeStruct((NB, NB), F32),) * outs,
-        in_specs=[VMEM] * len(args),
+        in_specs=[pl.BlockSpec(memory_space=pltpu.SMEM)] * len(place) + [VMEM] * len(args),
         out_specs=(VMEM,) * outs,
         scratch_shapes=[pltpu.VMEM((NB, NB), F32)] * held + [pltpu.VMEM((TILE, TILE), F32)] * 3,
         compiler_params=pltpu.CompilerParams(vmem_limit_bytes=24 << 20),
         cost_estimate=pl.CostEstimate(flops=30_000_000_000, bytes_accessed=len(args) << 20, transcendentals=0),
         name=name,
-    )(*args)
-
-
-def factor_all(a00, a10, a11):
-    state = squares(open_kernel, "open", 4, 0, a00)
-    l0, x0, _, l10, _, rest = squares(below_kernel, "below", 6, 1, *state, a10, a11)
-    state = squares(open_kernel, "open", 4, 0, rest)
-    l1, x1, _ = squares(close_kernel, "close", 3, 1, *state)
-    zero = jnp.zeros_like(l0)
-    x10 = -jnp.dot(x1, jnp.dot(l10, x0, precision="highest"), precision="highest")
-    return jnp.block([[l0, zero], [l10, l1]]), jnp.block([[x0, zero], [x10, x1]])
-
-
-def solve_kernel(col_ref, g0, g1, inv0, inv0_t, below, below_t, inv1, inv1_t, wh, wl, y, mid):
+    )(*place, *args)
+
+
+def solve_kernel(col_ref, g0, g1, inv0, inv0_t, below, below_t, inv1, inv1_t, parts, y, mid):
     col = col_ref[0]
+
+    def put(at, value):
+        high, low = split(value)
+        for k, part in enumerate((high, low, high)):
+            parts[k * EDGE + at : k * EDGE + at + NB, :] = part
+
     half = NB // 2
     y0 = jnp.concatenate([dot3(inv0[0:half, 0:half], g0[0:half, :]), dot3(inv0[half:, :], g0[...])], axis=0)
     rest = g1[...] - dot3(below[...], y0)
@@ -206,17 +244,13 @@
     w1 = jnp.concatenate(
         [dot3(inv1_t[0:half, :], mid[NB:, :]), dot3(inv1_t[half:, half:], mid[NB + half :, :])], axis=0
     )
-    h, l = split(w1)
-    wh[NB:, :] = h
-    wl[NB:, :] = l
+    put(NB, w1)
     z0 = mid[0:NB, :] - dot3(below_t[...], w1)
     w0 = jnp.concatenate([dot3(inv0_t[0:half, :], z0), dot3(inv0_t[half:, half:], z0[half:, :])], axis=0)
-    h, l = split(w0)
-    wh[0:NB, :] = h
-    wl[0:NB, :] = l
-
-
-def update_kernel(place, wh, wl, special, y, *refs):
+    put(0, w0)
+
+
+def update_kernel(place, weights, special, y, *refs):
     a_refs, b_refs = refs[0:5], refs[5:10]
     mat, rhs, out, out_rhs, rbuf, mbuf, vbuf, obuf, qbuf, rsem, msem, vsem, osem, qsem = refs[10:]
     row, col, here_z, here_y = place[0], place[1], place[2], place[3]
@@ -268,7 +302,7 @@
             drain(slot)
 
         rh, rl = split(rbuf[slot])
-        acc = mul(rh, wh[...]) + (mul(rh, wl[...]) + mul(rl, wh[...]))
+        acc = mul(jnp.concatenate([rh, rh, rl], axis=1), weights[...])
         obuf[slot] = jnp.where(col < 2, F32(0), mbuf[slot]) - acc[:, 0:NB]
         qbuf[slot] = vbuf[slot] - acc[:, NB:]
         for k in range(4):
@@ -291,9 +325,32 @@
 
 
 def ordered(parts, first):
-    both = jnp.concatenate(parts + parts, axis=0)
-    size = parts[0].shape[0]
-    return lax.dynamic_slice_in_dim(both, (4 - first) % 4 * size, 4 * size, 0)
+    return jnp.concatenate([lax.select_n(first, *(parts[(m - f) % 4] for f in range(4))) for m in range(4)], axis=0)
+
+
+def join_kernel(*refs):
+    parts, (first, second), sems = refs[:8], refs[8:10], refs[10]
+    copies = []
+    for k in range(8):
+        target = (first, second)[k // 4].at[pl.ds(k % 4 * TILE, TILE)]
+        copies.append(pltpu.make_async_copy(parts[k], target, sems.at[k]))
+    for copy in copies:
+        copy.start()
+    for copy in copies:
+        copy.wait()
+
+
+def join(*parts):
+    anywhere = pl.BlockSpec(memory_space=pl.ANY)
+    return pl.pallas_call(
+        join_kernel,
+        out_shape=(jax.ShapeDtypeStruct((4 * TILE, EDGE), F32),) * 2,
+        in_specs=[anywhere] * 8,
+        out_specs=(anywhere,) * 2,
+        scratch_shapes=[pltpu.SemaphoreType.DMA((8,))],
+        cost_estimate=pl.CostEstimate(flops=0, bytes_accessed=8 << 20, transcendentals=0),
+        name="join",
+    )(*parts)
 
 
 def turn_kernel(source, target):
@@ -370,7 +427,7 @@
     for d in (1, 2, 3):
         every = every + send(mine, lambda X, Y, Z, C, d=d: (X, d, Z, C) if Y == 0 else None)
     got += [strew(2), strew(3)]
-    every, *got = tie(every, *got)
+    (every,) = tie(every)
 
     zs = [every] + [send(every, ring("z", d)) for d in (1, 2, 3)]
     u = jnp.bitwise_xor(y % 2, x % 2)
@@ -378,38 +435,37 @@
     pick = lambda a, b, p: jnp.where(a == 0, jnp.where(b == 0, p[0], p[1]), jnp.where(b == 0, p[2], p[3]))
     piece = jnp.concatenate([pick(u, v, got), pick(1 - u, 1 - v, got)], axis=1)
     piece_a, piece_b = piece[0:TILE], piece[TILE:]
+    ring_z = ordered(zs, z)
+    ring_z, piece_a, piece_b = tie(ring_z, piece_a, piece_b)
+
+    mains = [ring_z[0:part]] + [send(ring_z[0:part], lambda X, Y, Z, C, d=d: (X - d, Y, Z, C)) for d in (1, 2, 3)]
     a1, a3 = send(piece_a, ring("y", 1)), send(piece_a, ring("y", 3))
-    ring_z = ordered(zs, z)
-    ring_z, piece_a, piece_b, a1, a3 = tie(ring_z, piece_a, piece_b, a1, a3)
-
-    mains = [ring_z[0:part]] + [send(ring_z[0:part], lambda X, Y, Z, C, d=d: (X - d, Y, Z, C)) for d in (1, 2, 3)]
+    main = jnp.concatenate(mains, axis=0)
+    main, a1, a3, piece_a, piece_b = tie(main, a1, a3, piece_a, piece_b)
+    other_main = swap_cores(main)
     a2, b1 = send(piece_a, ring("y", 2)), send(piece_b, ring("z", 1))
-    main = ordered(mains, x)
-    main, a2, b1, piece_b = tie(main, a2, b1, piece_b)
-    other_main = swap_cores(main)
-    b3, b2 = send(piece_b, ring("z", 3)), send(piece_b, ring("z", 2))
-    a00 = jnp.where(core == 0, main, other_main)
-    a10 = jnp.where(core == 0, other_main, main)
     tail = ring_z[part:]
-    a00, tail = tie(a00, tail)
+    main, other_main, tail, a2, b1, piece_b = tie(main, other_main, tail, a2, b1, piece_b)
     corners = [tail] + [send(tail, lambda X, Y, Z, C, d=d: (X - d, Y, Z, C)) for d in (1, 2, 3)]
-
-    state = squares(open_kernel, "open0", 4, 0, a00)
+    b2, b3 = send(piece_b, ring("z", 2)), send(piece_b, ring("z", 3))
+
+    place = (jnp.stack([x, core]),)
+    state = squares(first_kernel, "open0", 4, 0, main, other_main, place=place)
 
     state, b2, b3, corners = tie(state, b2, b3, corners)
-    corner = ordered(corners, x)
+    corner = jnp.concatenate(corners, axis=0)
     other_corner = swap_cores(corner)
-    a11 = jnp.where(core == 0, other_corner, corner)
-    rows_a = jnp.concatenate([piece_a, a1, a2, a3], axis=0)
-    rows_b = jnp.concatenate([piece_b, b1, b2, b3], axis=0)
+    rows_a, rows_b = join(piece_a, a1, a2, a3, piece_b, b1, b2, b3)
     fars = []
     for rows, axis in ((rows_a, "z"), (rows_b, "y")):
         fars.append((send(rows, ring(axis, 1)), send(rows, ring(axis, 3))))
-    first_rows, top_rhs, a11 = tie(first, right_sides[0:NB], a11)
+    first_rows, top_rhs, other_corner = tie(first, right_sides[0:NB], other_corner)
 
     top = jnp.concatenate([first_rows, top_rhs], axis=1)
     crossed = send(top, lambda X, Y, Z, C: (X + 1, Y, Z, C) if X % 2 == 0 else None)
-    l0, inv0, inv0_t, below, below_t, rest = squares(below_kernel, "below0", 6, 1, *state, a10, a11)
+    l0, inv0, inv0_t, below, below_t, rest = squares(
+        below_kernel, "below0", 6, 1, *state, main, other_main, corner, other_corner, place=place
+    )
     state = squares(open_kernel, "open1", 4, 0, rest)
 
     state, fars, crossed = tie(state, fars, crossed)
@@ -426,15 +482,14 @@
     g1 = jnp.where(core == 0, partner, own)
 
     width = NB + right_sides.shape[1]
-    wh, wl, answer = pl.pallas_call(
+    weights, answer = pl.pallas_call(
         solve_kernel,
         out_shape=(
-            jax.ShapeDtypeStruct((EDGE, width), BF16),
-            jax.ShapeDtypeStruct((EDGE, width), BF16),
+            jax.ShapeDtypeStruct((3 * EDGE, width), BF16),
             jax.ShapeDtypeStruct((EDGE, width - NB), F32),
         ),
         in_specs=[pl.BlockSpec(memory_space=pltpu.SMEM)] + [VMEM] * 8,
-        out_specs=(VMEM,) * 3,
+        out_specs=(VMEM,) * 2,
         scratch_shapes=[pltpu.VMEM((EDGE, width), F32)],
         compiler_params=pltpu.CompilerParams(vmem_limit_bytes=48 << 20),
         cost_estimate=pl.CostEstimate(flops=10_000_000_000, bytes_accessed=16 << 20, transcendentals=0),
@@ -449,7 +504,7 @@
     pair = lambda *shape: pltpu.VMEM((2,) + shape, F32)
     return pl.pallas_call(
         update_kernel,
-        in_specs=[pl.BlockSpec(memory_space=pltpu.SMEM)] + [VMEM] * 4 + [anywhere] * 12,
+        in_specs=[pl.BlockSpec(memory_space=pltpu.SMEM)] + [VMEM] * 3 + [anywhere] * 12,
         out_specs=(anywhere, anywhere),
         out_shape=(
             jax.ShapeDtypeStruct(matrix.shape, F32),
@@ -466,7 +521,7 @@
         compiler_params=pltpu.CompilerParams(vmem_limit_bytes=48 << 20),
         cost_estimate=pl.CostEstimate(flops=20_000_000_000, bytes_accessed=44 << 20, transcendentals=0),
         name="update",
-    )(jnp.stack([row, col, z, y]), wh, wl, special, answer, *gathered, matrix, right_sides)
+    )(jnp.stack([row, col, z, y]), weights, special, answer, *gathered, matrix, right_sides)
 
 
 def solution(mesh):

time: 279 us -> 389 us (1.39)
  Pallas kernels: 127 us -> 240 us
  waiting for transfers between devices: 35.3 us -> 50.5 us
  starting transfers between devices: 80.1 us -> 64.9 us
  local copies, waits for them, and re-layouts: 21.8 us -> 17.1 us
    pallas_call x1 -> x2, Pallas kernels: 11.5 us -> 140 us  [the longest x1 128 us: join(): pl.pallas_call(join_kernel, out_shape=(jax.ShapeDtypeStruct((4 * TILE, ED...]
    pallas_call x4, Pallas kernels: 87.5 us -> 72.2 us  [squares(): pl.pallas_call(kernel, out_shape=(jax.ShapeDtypeStruct((NB, NB), F32),) *...]
    ppermute x40, waiting for transfers between devices: 35.3 us -> 50.5 us  [send(): return lax.ppermute(value, AXES, route(rule))]
    ppermute x40, starting transfers between devices: 80.1 us -> 64.9 us  [send(): return lax.ppermute(value, AXES, route(rule))]
    unnamed x78 -> x54, local copies, waits for them, and re-layouts: 14.3 us -> 7.64 us
  transfers between devices with their start and end apart: 40 -> 40, of which waited for: 12 -> 13; matrix products, arithmetic and copies ran while one was open for 7% -> 2% of each run, Pallas kernels for 36% -> 56%
where the time goes in v3:
time: 389 us; the launch traced here: 382 us
  Pallas kernels  240 us (62%)
  starting transfers between devices  64.9 us (17%)
  waiting for transfers between devices  50.5 us (13%)
  local copies, waits for them, and re-layouts  17.1 us (4%)
  other arithmetic  7.43 us (2%)
    pallas_call x1, Pallas kernels, join(): pl.pallas_call(join_kernel, out_shape=(jax.ShapeDtypeStruct((4 * TILE, ED...  128 us
    pallas_call x4, Pallas kernels, squares(): pl.pallas_call(kernel, out_shape=(jax.ShapeDtypeStruct((NB, NB), F32),) *...  72.2 us
    ppermute x40, starting transfers between devices, send(): return lax.ppermute(value, AXES, route(rule))  64.9 us
    ppermute x40, waiting for transfers between devices, send(): return lax.ppermute(value, AXES, route(rule))  50.5 us
    pallas_call x1, Pallas kernels, body(): pl.pallas_call(update_kernel, in_specs=[pl.BlockSpec(memory_space=pltpu.S...  27.7 us
    pallas_call x1, Pallas kernels, body(): pl.pallas_call(solve_kernel, out_shape=(jax.ShapeDtypeStruct((3 * EDGE, w...  12 us
  transfers between devices with their start and end apart: 40, of which 13 were waited for; matrix products, arithmetic and copies ran while one was open for 2% of the time, Pallas kernels for 56%

profile of v3, /device:TPU:1, one launch (start us, length us, event | category | flops | bytes accessed | tf_op | source)
XLA Modules:
  0.0 382.0 jit_solution(1069044006136671962)
XLA Ops:
  2.0 4.0 %collective-permute-start = (f32[128,512]{1,0:T(8,128)S(1)}, f32[128,512]{1,0:T(8,128)S(1)}, u32[]{:S(2)}, u32[]{:S(2)}) collective-permute-start(f32[128,512]{1,0:T(8,128)S(1)} %get-tuple-element.136), channel_id=1, source_target_pairs={{0,64},{32,96},{1,65},{33,97}} | collective-permute-start | bytes 786440 | tf_op jit(solution)/shard_map/ppermute | solution.py:37
  6.0 2.6 collective-permute-start.2
  8.6 3.1 collective-permute-start.1
  13.5 6.6 %collective-permute-done.1 = f32[128,512]{1,0:T(8,128)} collective-permute-done((f32[128,512]{1,0:T(8,128)S(1)}, f32[128,512]{1,0:T(8,128)}, u32[]{:S(2)}, u32[]{:S(2)}) %collective-permute-start.1) | collective-permute-done | bytes 262176 | tf_op jit(solution)/shard_map/ppermute | solution.py:37
  23.2 2.1 collective-permute-start.6
  28.7 1.9 collective-permute-start.4
  34.2 4.2 %collective-permute-done.7 = f32[256,512]{1,0:T(8,128)} collective-permute-done((f32[256,512]{1,0:T(8,128)S(1)}, f32[256,512]{1,0:T(8,128)}, u32[]{:S(2)}, u32[]{:S(2)}) %collective-permute-start.7) | collective-permute-done | bytes 524320 | tf_op jit(solution)/shard_map/ppermute | solution.py:37
  42.3 2.0 collective-permute-start.8
  45.7 4.3 %collective-permute-start.14 = (f32[256,512]{1,0:T(8,128)S(1)}, f32[256,512]{1,0:T(8,128)S(1)}, u32[]{:S(2)}, u32[]{:S(2)}) collective-permute-start(f32[256,512]{1,0:T(8,128)S(1)} %constant_dynamic-slice_fusion.1), channel_id=1, source_target_pairs={{0,2},{32,1},{8,10},{40,9},{16,18},{48,17},{24,26},{56,25},{2,64},... | collective-permute-start | bytes 1572872 | tf_op jit(solution)/shard_map/ppermute | solution.py:37
  52.6 3.8 %collective-permute-done.13 = f32[64,512]{1,0:T(8,128)S(1)} collective-permute-done((f32[64,512]{1,0:T(8,128)S(1)}, f32[64,512]{1,0:T(8,128)S(1)}, u32[]{:S(2)}, u32[]{:S(2)}) %collective-permute-start.13) | collective-permute-done | bytes 131104 | tf_op jit(solution)/shard_map/ppermute | solution.py:37
  57.0 2.4 collective-permute-done.11
  62.1 2.7 collective-permute-start.19
  66.2 2.0 collective-permute-start.16
  68.2 11.2 %collective-permute-done.18 = f32[128,512]{1,0:T(8,128)S(1)} collective-permute-done((f32[128,512]{1,0:T(8,128)S(1)}, f32[128,512]{1,0:T(8,128)S(1)}, u32[]{:S(2)}, u32[]{:S(2)}) %collective-permute-start.18) | collective-permute-done | bytes 262176 | tf_op jit(solution)/shard_map/ppermute | solution.py:37
  81.3 14.9 %collective-permute-done.22.refs_2_ = f32[128,1024]{1,0:T(8,128)S(1)} collective-permute-done((f32[128,1024]{1,0:T(8,128)S(1)}, f32[128,1024]{1,0:T(8,128)S(1)}, u32[]{:S(2)}, u32[]{:S(2)}) %collective-permute-start.22) | collective-permute-done | bytes 524320 | tf_op jit(solution)/shard_map/ppermute | solution.py:37
  96.9 2.9 collective-permute-start.27
  99.9 2.1 collective-permute-start.24
  102.0 17.0 %open0.1 = (f32[512,512]{1,0:T(8,128)S(1)}, f32[512,512]{1,0:T(8,128)S(1)}, f32[512,512]{1,0:T(8,128)S(1)}, f32[512,512]{1,0:T(8,128)S(1)}) custom-call(s32[2]{0:T(128)S(1)} %pad_add_fusion.1.place, f32[512,512]{1,0:T(8,128)S(1)} %pad_maximum_fusion.mine, f32[512,512]{1,0:T(8,128)S(1)} %collective-permute-done.21.other), custom_call_target="tpu_custom_call" | custom-call | flops 30000001024 | bytes 2097152 | tf_op jit(solution)/shard_map/open0/pallas_call | solution.py:211
  121.0 2.1 collective-permute-done.24.refs_6_
  124.0 3.7 collective-permute-start.29
  129.6 128.2 %join.1 = (f32[512,1024]{1,0:T(8,128)}, f32[512,1024]{1,0:T(8,128)}) custom-call(f32[128,1024]{1,0:T(8,128)} %copy-done.13, f32[128,1024]{1,0:T(8,128)} %copy-done.19, f32[128,1024]{1,0:T(8,128)} %copy-done.20, f32[128,1024]{1,0:T(8,128)} %copy-done.18, f32[128,1024]{1,0:T(8,128)} %copy-done.12, f32[128,1024]{1,0:T(8,128)} %copy-done.21, ...), custom_call_target="tpu_custom_call" | custom-call | bytes 8388608 | tf_op jit(solution)/shard_map/join/pallas_call | solution.py:345
  257.9 2.7 collective-permute-start.30
  260.6 2.7 collective-permute-start.32
  264.5 3.5 collective-permute-start.34
  270.4 21.9 %below0.1 = (f32[512,512]{1,0:T(8,128)S(1)}, f32[512,512]{1,0:T(8,128)S(1)}, f32[512,512]{1,0:T(8,128)S(1)}, f32[512,512]{1,0:T(8,128)S(1)}, f32[512,512]{1,0:T(8,128)S(1)}, /*index=5*/f32[512,512]{1,0:T(8,128)S(1)}) custom-call(s32[2]{0:T(128)S(1)} %pad_add_fusion.1.place, f32[512,512]{1,0:T(8,128)S(1)} %copy-done.5, f32[512,512]{1,0:T(8,128)S(1)} %copy-done.7, ...), custom_call_target="tpu_custom_call" | custom-call | flops 30000001024 | bytes 8388608 | tf_op jit(solution)/shard_map/below0/pallas_call | solution.py:211
  292.3 16.4 %open1.1 = (f32[512,512]{1,0:T(8,128)S(1)}, f32[512,512]{1,0:T(8,128)S(1)}, f32[512,512]{1,0:T(8,128)S(1)}, f32[512,512]{1,0:T(8,128)S(1)}) custom-call(f32[512,512]{1,0:T(8,128)S(1)} %get-tuple-element.96.source), custom_call_target="tpu_custom_call" | custom-call | flops 30000001024 | bytes 1048576 | tf_op jit(solution)/shard_map/open1/pallas_call | solution.py:211
  313.8 2.7 collective-permute-start.38
  316.5 2.7 collective-permute-start.36
  319.3 2.6 collective-permute-start.35
  321.9 16.8 %close1.1 = (f32[512,512]{1,0:T(8,128)S(1)}, f32[512,512]{1,0:T(8,128)S(1)}, f32[512,512]{1,0:T(8,128)S(1)}) custom-call(f32[512,512]{1,0:T(8,128)S(1)} %get-tuple-element.114.m, f32[512,512]{1,0:T(8,128)S(1)} %get-tuple-element.115.l, f32[512,512]{1,0:T(8,128)S(1)} %get-tuple-element.116.i, f32[512,512]{1,0:T(8,128)S(1)} %get-tuple-element.117.t), custom_call_target="tpu_custom_call" | custom-call | flops 30000001024 | bytes 4194304 | tf_op jit(solution)/shard_map/close1/pallas_call | solution.py:211
  342.0 12.0 %solve.1 = (bf16[3072,768]{1,0:T(8,128)(2,1)}, f32[1024,256]{1,0:T(8,128)S(1)}) custom-call(s32[1]{0:T(128)} %bitcast.1.col_ref, f32[512,768]{1,0:T(8,128)} %get-tuple-element.129.g0, f32[512,768]{1,0:T(8,128)} %get-tuple-element.128.g1, f32[512,512]{1,0:T(8,128)S(1)} %get-tuple-element.110.inv0, f32[512,512]{1,0:T(8,128)S(1)} %get-tuple-element.111.inv0_t, ...), custom_call_target="tpu_custom_call" | custom-call | flops 10000000000 | bytes 16777216 | tf_op jit(solution)/shard_map/solve/pallas_call | solution.py:485
  354.1 27.7 %update.1 = (f32[4096,512]{1,0:T(8,128)}, f32[4096,256]{1,0:T(8,128)}) custom-call(s32[4]{0:T(128)S(1)} %pad_add_fusion.place, bf16[3072,768]{1,0:T(8,128)(2,1)} %get-tuple-element.120.weights, f32[512,512]{1,0:T(8,128)S(1)} %select_select_fusion.special, f32[512,256]{1,0:T(8,128)S(1)} %constant_dynamic-slice_fusion.y, ...), custom_call_target="tpu_custom_call" | custom-call | flops 20000000000 | bytes 46137344 | tf_op jit(solution)/shard_map/update/pallas_call | solution.py:505
  (138 shorter events, 44.9 us)
Async XLA Ops:
  2.0 10.1 %collective-permute-start = (f32[128,512]{1,0:T(8,128)S(1)}, f32[128,512]{1,0:T(8,128)S(1)}, u32[]{:S(2)}, u32[]{:S(2)}) collective-permute-start(f32[128,512]{1,0:T(8,128)S(1)} %get-tuple-element.136), channel_id=1, source_target_pairs={{0,64},{32,96},{1,65},{33,97}} | collective-permute-start | bytes 786440 | tf_op jit(solution)/shard_map/ppermute | solution.py:37
  8.6 11.6 %collective-permute-start.1 = (f32[128,512]{1,0:T(8,128)S(1)}, f32[128,512]{1,0:T(8,128)}, u32[]{:S(2)}, u32[]{:S(2)}) collective-permute-start(f32[128,512]{1,0:T(8,128)S(1)} %get-tuple-element.138), channel_id=1, source_target_pairs={{0,1},{32,33},{1,0},{33,32}} | collective-permute-start | bytes 786440 | tf_op jit(solution)/shard_map/ppermute | solution.py:37
  21.3 17.2 %collective-permute-start.7 = (f32[256,512]{1,0:T(8,128)S(1)}, f32[256,512]{1,0:T(8,128)}, u32[]{:S(2)}, u32[]{:S(2)}) collective-permute-start(f32[256,512]{1,0:T(8,128)S(1)} %constant_dynamic-slice_fusion.2), channel_id=1, source_target_pairs={{0,1},{32,2},{8,9},{40,10},{16,17},{48,18},{24,25},{56,26},{2,67},... | collective-permute-start | bytes 1572872 | tf_op jit(solution)/shard_map/ppermute | solution.py:37
  23.2 15.3 %collective-permute-start.6 = (f32[256,512]{1,0:T(8,128)S(1)}, f32[256,512]{1,0:T(8,128)}, u32[]{:S(2)}, u32[]{:S(2)}) collective-permute-start(f32[256,512]{1,0:T(8,128)S(1)} %constant_dynamic-slice_fusion.2), channel_id=1, source_target_pairs={{0,0},{32,3},{8,8},{40,11},{16,16},{48,19},{24,24},{56,27},{2,66},... | collective-permute-start | bytes 1572872 | tf_op jit(solution)/shard_map/ppermute | solution.py:37
  38.5 11.5 %collective-permute-start.10 = (f32[64,512]{1,0:T(8,128)S(1)}, f32[64,512]{1,0:T(8,128)}, u32[]{:S(2)}, u32[]{:S(2)}) collective-permute-start(f32[64,512]{1,0:T(8,128)S(1)} %add_add_fusion.1), channel_id=1, source_target_pairs={{0,6},{32,38},{8,14},{40,46},{16,22},{48,54},{24,30},{56,62},{64,7... | collective-permute-start | bytes 393224 | tf_op jit(solution)/shard_map/ppermute | solution.py:37
  40.4 9.6 %collective-permute-start.9 = (f32[64,512]{1,0:T(8,128)S(1)}, f32[64,512]{1,0:T(8,128)}, u32[]{:S(2)}, u32[]{:S(2)}) collective-permute-start(f32[64,512]{1,0:T(8,128)S(1)} %add_add_fusion.1), channel_id=1, source_target_pairs={{0,4},{32,36},{8,12},{40,44},{16,20},{48,52},{24,28},{56,60},{64,6... | collective-permute-start | bytes 393224 | tf_op jit(solution)/shard_map/ppermute | solution.py:37
  44.4 15.2 %collective-permute-start.15 = (f32[256,512]{1,0:T(8,128)S(1)}, f32[256,512]{1,0:T(8,128)S(1)}, u32[]{:S(2)}, u32[]{:S(2)}) collective-permute-start(f32[256,512]{1,0:T(8,128)S(1)} %constant_dynamic-slice_fusion.1), channel_id=1, source_target_pairs={{0,3},{32,0},{8,11},{40,8},{16,19},{48,16},{24,27},{56,24},{2,65},... | collective-permute-start | bytes 1572872 | tf_op jit(solution)/shard_map/ppermute | solution.py:37
  45.7 14.8 %collective-permute-start.14 = (f32[256,512]{1,0:T(8,128)S(1)}, f32[256,512]{1,0:T(8,128)S(1)}, u32[]{:S(2)}, u32[]{:S(2)}) collective-permute-start(f32[256,512]{1,0:T(8,128)S(1)} %constant_dynamic-slice_fusion.1), channel_id=1, source_target_pairs={{0,2},{32,1},{8,10},{40,9},{16,18},{48,17},{24,26},{56,25},{2,64},... | collective-permute-start | bytes 1572872 | tf_op jit(solution)/shard_map/ppermute | solution.py:37
  62.0 17.7 %collective-permute-start.20 = (f32[128,1024]{1,0:T(8,128)S(1)}, f32[128,1024]{1,0:T(8,128)S(1)}, u32[]{:S(2)}, u32[]{:S(2)}) collective-permute-start(f32[128,1024]{1,0:T(8,128)S(1)} %get-tuple-element.75.refs_0_), channel_id=1, source_target_pairs={{0,2},{32,34},{8,10},{40,42},{16,18},{48,50},{24,26},{56,58},{2,4}... | collective-permute-start | bytes 1572872 | tf_op jit(solution)/shard_map/ppermute | solution.py:37
  62.1 17.7 %collective-permute-start.19 = (f32[128,1024]{1,0:T(8,128)S(1)}, f32[128,1024]{1,0:T(8,128)S(1)}, u32[]{:S(2)}, u32[]{:S(2)}) collective-permute-start(f32[128,1024]{1,0:T(8,128)S(1)} %get-tuple-element.75.refs_0_), channel_id=1, source_target_pairs={{0,6},{32,38},{8,14},{40,46},{16,22},{48,54},{24,30},{56,62},{2,0}... | collective-permute-start | bytes 1572872 | tf_op jit(solution)/shard_map/ppermute | solution.py:37
  64.8 14.6 %collective-permute-start.18 = (f32[128,512]{1,0:T(8,128)S(1)}, f32[128,512]{1,0:T(8,128)S(1)}, u32[]{:S(2)}, u32[]{:S(2)}) collective-permute-start(f32[128,512]{1,0:T(8,128)S(1)} %get-tuple-element.140), channel_id=1, source_target_pairs={{0,64},{32,96},{8,72},{40,104},{16,80},{48,112},{24,88},{56,120},{... | collective-permute-start | bytes 786440 | tf_op jit(solution)/shard_map/ppermute | solution.py:37
  64.9 14.5 %collective-permute-start.17 = (f32[128,512]{1,0:T(8,128)S(1)}, f32[128,512]{1,0:T(8,128)S(1)}, u32[]{:S(2)}, u32[]{:S(2)}) collective-permute-start(f32[128,512]{1,0:T(8,128)S(1)} %get-tuple-element.140), channel_id=1, source_target_pairs={{0,1},{32,33},{8,9},{40,41},{16,17},{48,49},{24,25},{56,57},{2,3},... | collective-permute-start | bytes 786440 | tf_op jit(solution)/shard_map/ppermute | solution.py:37
  66.2 13.5 %collective-permute-start.16 = (f32[128,512]{1,0:T(8,128)S(1)}, f32[128,512]{1,0:T(8,128)S(1)}, u32[]{:S(2)}, u32[]{:S(2)}) collective-permute-start(f32[128,512]{1,0:T(8,128)S(1)} %get-tuple-element.140), channel_id=1, source_target_pairs={{0,65},{32,97},{8,73},{40,105},{16,81},{48,113},{24,89},{56,121},{... | collective-permute-start | bytes 786440 | tf_op jit(solution)/shard_map/ppermute | solution.py:37
  79.8 16.4 %collective-permute-start.21 = (f32[512,512]{1,0:T(8,128)S(1)}, f32[512,512]{1,0:T(8,128)S(1)}, u32[]{:S(2)}, u32[]{:S(2)}) collective-permute-start(f32[512,512]{1,0:T(8,128)S(1)} %pad_maximum_fusion.mine), channel_id=1, source_target_pairs={{0,32},{32,0},{8,40},{40,8},{16,48},{48,16},{24,56},{56,24},{2,34}... | collective-permute-start | bytes 3145736 | tf_op jit(solution)/shard_map/ppermute | solution.py:37
  81.2 15.0 %collective-permute-start.22 = (f32[128,1024]{1,0:T(8,128)S(1)}, f32[128,1024]{1,0:T(8,128)S(1)}, u32[]{:S(2)}, u32[]{:S(2)}) collective-permute-start(f32[128,1024]{1,0:T(8,128)S(1)} %get-tuple-element.75.refs_0_), channel_id=1, source_target_pairs={{0,4},{32,36},{8,12},{40,44},{16,20},{48,52},{24,28},{56,60},{2,6}... | collective-permute-start | bytes 1572872 | tf_op jit(solution)/shard_map/ppermute | solution.py:37
  81.2 15.0 %collective-permute-start.23 = (f32[128,1024]{1,0:T(8,128)S(1)}, f32[128,1024]{1,0:T(8,128)S(1)}, u32[]{:S(2)}, u32[]{:S(2)}) collective-permute-start(f32[128,1024]{1,0:T(8,128)S(1)} %get-tuple-element.83.refs_4_), channel_id=1, source_target_pairs={{0,24},{32,56},{8,0},{40,32},{16,8},{48,40},{24,16},{56,48},{2,26}... | collective-permute-start | bytes 1572872 | tf_op jit(solution)/shard_map/ppermute | solution.py:37
  96.2 24.8 %collective-permute-start.28 = (f32[128,512]{1,0:T(8,128)S(1)}, f32[128,512]{1,0:T(8,128)S(1)}, u32[]{:S(2)}, u32[]{:S(2)}) collective-permute-start(f32[128,512]{1,0:T(8,128)S(1)} %get-tuple-element.85), channel_id=1, source_target_pairs={{0,64},{32,96},{8,72},{40,104},{16,80},{48,112},{24,88},{56,120},{... | collective-permute-start | bytes 786440 | tf_op jit(solution)/shard_map/ppermute | solution.py:37
  96.9 24.1 %collective-permute-start.27 = (f32[128,512]{1,0:T(8,128)S(1)}, f32[128,512]{1,0:T(8,128)S(1)}, u32[]{:S(2)}, u32[]{:S(2)}) collective-permute-start(f32[128,512]{1,0:T(8,128)S(1)} %get-tuple-element.85), channel_id=1, source_target_pairs={{0,1},{32,33},{8,9},{40,41},{16,17},{48,49},{24,25},{56,57},{2,3},... | collective-permute-start | bytes 786440 | tf_op jit(solution)/shard_map/ppermute | solution.py:37
  99.8 21.2 %collective-permute-start.26 = (f32[128,512]{1,0:T(8,128)S(1)}, f32[128,512]{1,0:T(8,128)S(1)}, u32[]{:S(2)}, u32[]{:S(2)}) collective-permute-start(f32[128,512]{1,0:T(8,128)S(1)} %get-tuple-element.85), channel_id=1, source_target_pairs={{0,65},{32,97},{8,73},{40,105},{16,81},{48,113},{24,89},{56,121},{... | collective-permute-start | bytes 786440 | tf_op jit(solution)/shard_map/ppermute | solution.py:37
  99.9 21.2 %collective-permute-start.25 = (f32[128,1024]{1,0:T(8,128)S(1)}, f32[128,1024]{1,0:T(8,128)S(1)}, u32[]{:S(2)}, u32[]{:S(2)}) collective-permute-start(f32[128,1024]{1,0:T(8,128)S(1)} %get-tuple-element.83.refs_4_), channel_id=1, source_target_pairs={{0,8},{32,40},{8,16},{40,48},{16,24},{48,56},{24,0},{56,32},{2,10}... | collective-permute-start | bytes 1572872 | tf_op jit(solution)/shard_map/ppermute | solution.py:37
  99.9 23.3 %collective-permute-start.24 = (f32[128,1024]{1,0:T(8,128)S(1)}, f32[128,1024]{1,0:T(8,128)S(1)}, u32[]{:S(2)}, u32[]{:S(2)}) collective-permute-start(f32[128,1024]{1,0:T(8,128)S(1)} %get-tuple-element.83.refs_4_), channel_id=1, source_target_pairs={{0,16},{32,48},{8,24},{40,56},{16,0},{48,32},{24,8},{56,40},{2,18}... | collective-permute-start | bytes 1572872 | tf_op jit(solution)/shard_map/ppermute | solution.py:37
  124.0 139.3 %collective-permute-start.29 = (f32[512,512]{1,0:T(8,128)S(1)}, f32[512,512]{1,0:T(8,128)}, u32[]{:S(2)}, u32[]{:S(2)}) collective-permute-start(f32[512,512]{1,0:T(8,128)S(1)} %constant_dynamic-update-slice_fusion.edge), channel_id=1, source_target_pairs={{0,32},{32,0},{8,40},{40,8},{16,48},{48,16},{24,56},{56,24},{2,34}... | collective-permute-start | bytes 3145736 | tf_op jit(solution)/shard_map/ppermute | solution.py:37
  257.9 50.9 %collective-permute-start.31 = (f32[512,1024]{1,0:T(8,128)}, f32[512,1024]{1,0:T(8,128)S(1)}, u32[]{:S(2)}, u32[]{:S(2)}) collective-permute-start(f32[512,1024]{1,0:T(8,128)} %get-tuple-element.107.refs_0_), channel_id=1, source_target_pairs={{0,8},{32,40},{8,16},{40,48},{16,24},{48,56},{24,0},{56,32},{2,10}... | collective-permute-start | bytes 6291464 | tf_op jit(solution)/shard_map/ppermute | solution.py:37
  257.9 50.8 %collective-permute-start.30 = (f32[512,1024]{1,0:T(8,128)}, f32[512,1024]{1,0:T(8,128)S(1)}, u32[]{:S(2)}, u32[]{:S(2)}) collective-permute-start(f32[512,1024]{1,0:T(8,128)} %get-tuple-element.107.refs_0_), channel_id=1, source_target_pairs={{0,24},{32,56},{8,0},{40,32},{16,8},{48,40},{24,16},{56,48},{2,26}... | collective-permute-start | bytes 6291464 | tf_op jit(solution)/shard_map/ppermute | solution.py:37
  260.6 48.2 %collective-permute-start.33 = (f32[512,1024]{1,0:T(8,128)}, f32[512,1024]{1,0:T(8,128)S(1)}, u32[]{:S(2)}, u32[]{:S(2)}) collective-permute-start(f32[512,1024]{1,0:T(8,128)} %get-tuple-element.108.refs_5_), channel_id=1, source_target_pairs={{0,2},{32,34},{8,10},{40,42},{16,18},{48,50},{24,26},{56,58},{2,4}... | collective-permute-start | bytes 6291464 | tf_op jit(solution)/shard_map/ppermute | solution.py:37
  260.6 48.2 %collective-permute-start.32 = (f32[512,1024]{1,0:T(8,128)}, f32[512,1024]{1,0:T(8,128)S(1)}, u32[]{:S(2)}, u32[]{:S(2)}) collective-permute-start(f32[512,1024]{1,0:T(8,128)} %get-tuple-element.108.refs_5_), channel_id=1, source_target_pairs={{0,6},{32,38},{8,14},{40,46},{16,22},{48,54},{24,30},{56,62},{2,0}... | collective-permute-start | bytes 6291464 | tf_op jit(solution)/shard_map/ppermute | solution.py:37
  264.5 44.4 %collective-permute-start.34 = (f32[512,768]{1,0:T(8,128)S(1)}, f32[512,768]{1,0:T(8,128)S(1)}, u32[]{:S(2)}, u32[]{:S(2)}) collective-permute-start(f32[512,768]{1,0:T(8,128)S(1)} %constant_dynamic-update-slice_fusion.4), channel_id=1, source_target_pairs={{0,64},{32,96},{8,72},{40,104},{16,80},{48,112},{24,88},{56,120},{... | collective-permute-start | bytes 4718600 | tf_op jit(solution)/shard_map/ppermute | solution.py:37
  313.8 40.3 %collective-permute-start.39 = (f32[256,1024]{1,0:T(8,128)}, f32[256,1024]{1,0:T(8,128)S(1)}, u32[]{:S(2)}, u32[]{:S(2)}) collective-permute-start(f32[256,1024]{1,0:T(8,128)} %slice.58), channel_id=1, source_target_pairs={{0,2},{32,34},{8,10},{40,42},{16,18},{48,50},{24,26},{56,58},{2,4}... | collective-permute-start | bytes 3145736 | tf_op jit(solution)/shard_map/ppermute | solution.py:37
  313.8 40.3 %collective-permute-start.38 = (f32[256,1024]{1,0:T(8,128)}, f32[256,1024]{1,0:T(8,128)S(1)}, u32[]{:S(2)}, u32[]{:S(2)}) collective-permute-start(f32[256,1024]{1,0:T(8,128)} %slice.57), channel_id=1, source_target_pairs={{0,6},{32,38},{8,14},{40,46},{16,22},{48,54},{24,30},{56,62},{2,0}... | collective-permute-start | bytes 3145736 | tf_op jit(solution)/shard_map/ppermute | solution.py:37
  316.5 37.6 %collective-permute-start.37 = (f32[256,1024]{1,0:T(8,128)}, f32[256,1024]{1,0:T(8,128)S(1)}, u32[]{:S(2)}, u32[]{:S(2)}) collective-permute-start(f32[256,1024]{1,0:T(8,128)} %slice.56), channel_id=1, source_target_pairs={{0,8},{32,40},{8,16},{40,48},{16,24},{48,56},{24,0},{56,32},{2,10}... | collective-permute-start | bytes 3145736 | tf_op jit(solution)/shard_map/ppermute | solution.py:37
  316.5 37.6 %collective-permute-start.36 = (f32[256,1024]{1,0:T(8,128)S(1)}, f32[256,1024]{1,0:T(8,128)S(1)}, u32[]{:S(2)}, u32[]{:S(2)}) collective-permute-start(f32[256,1024]{1,0:T(8,128)S(1)} %slice.55), channel_id=1, source_target_pairs={{0,24},{32,56},{8,0},{40,32},{16,8},{48,40},{24,16},{56,48},{2,26}... | collective-permute-start | bytes 3145736 | tf_op jit(solution)/shard_map/ppermute | solution.py:37
  319.3 20.8 %collective-permute-start.35 = (f32[512,768]{1,0:T(8,128)S(1)}, f32[512,768]{1,0:T(8,128)S(1)}, u32[]{:S(2)}, u32[]{:S(2)}) collective-permute-start(f32[512,768]{1,0:T(8,128)S(1)} %broadcast_select_fusion), channel_id=1, source_target_pairs={{0,32},{32,0},{8,40},{40,8},{16,48},{48,16},{24,56},{56,24},{2,34}... | collective-permute-start | bytes 4718600 | tf_op jit(solution)/shard_map/ppermute | solution.py:37
  (33 other events, 230.1 us)

commit v4 on v3

--- a/solution.py
+++ b/solution.py
@@ -176,7 +176,11 @@
     low[...] = jnp.zeros_like(low)
     inv[...] = jnp.zeros_like(inv)
     inv_t[...] = jnp.zeros_like(inv_t)
-    factor_blocks((0, 1), mat, low, inv, inv_t, work, tile_inv, tile_t)
+    factor_blocks((0,), mat, low, inv, inv_t, work, tile_inv, tile_t)
+
+
+def middle_kernel(m, l, i, t, mat, low, inv, inv_t, *tiles):
+    carry_on((1,), (m, l, i, t), mat, low, inv, inv_t, tiles)
 
 
 def open_kernel(source, mat, low, inv, inv_t, work, tile_inv, tile_t):
@@ -187,18 +191,18 @@
     factor_blocks((0, 1), mat, low, inv, inv_t, work, tile_inv, tile_t)
 
 
-def carry_on(sources, mat, low, inv, inv_t, tiles):
+def carry_on(blocks, sources, mat, low, inv, inv_t, tiles):
     for source, target in zip(sources, (mat, low, inv, inv_t)):
         target[...] = source[...]
-    factor_blocks((2, 3), mat, low, inv, inv_t, *tiles)
+    factor_blocks(blocks, mat, low, inv, inv_t, *tiles)
 
 
 def close_kernel(m, l, i, t, low, inv, inv_t, mat, *tiles):
-    carry_on((m, l, i, t), mat, low, inv, inv_t, tiles)
+    carry_on((2, 3), (m, l, i, t), mat, low, inv, inv_t, tiles)
 
 
 def below_kernel(place, m, l, i, t, mine, other, edge, far_edge, low, inv, inv_t, below, below_t, rest, mat, *tiles):
-    carry_on((m, l, i, t), mat, low, inv, inv_t, tiles)
+    carry_on((2, 3), (m, l, i, t), mat, low, inv, inv_t, tiles)
     place_quarters(place, mine, other, rest, 1)
     panel = dot_full(rest[...], inv_t[...])
     below[...] = panel
@@ -329,25 +333,18 @@
 
 
 def join_kernel(*refs):
-    parts, (first, second), sems = refs[:8], refs[8:10], refs[10]
-    copies = []
+    parts, joined = refs[:8], refs[8:]
     for k in range(8):
-        target = (first, second)[k // 4].at[pl.ds(k % 4 * TILE, TILE)]
-        copies.append(pltpu.make_async_copy(parts[k], target, sems.at[k]))
-    for copy in copies:
-        copy.start()
-    for copy in copies:
-        copy.wait()
+        joined[k // 4][k % 4 * TILE : (k % 4 + 1) * TILE, :] = parts[k][...]
 
 
 def join(*parts):
-    anywhere = pl.BlockSpec(memory_space=pl.ANY)
     return pl.pallas_call(
         join_kernel,
         out_shape=(jax.ShapeDtypeStruct((4 * TILE, EDGE), F32),) * 2,
-        in_specs=[anywhere] * 8,
-        out_specs=(anywhere,) * 2,
-        scratch_shapes=[pltpu.SemaphoreType.DMA((8,))],
+        in_specs=[VMEM] * 8,
+        out_specs=(VMEM,) * 2,
+        compiler_params=pltpu.CompilerParams(vmem_limit_bytes=12 << 20),
         cost_estimate=pl.CostEstimate(flops=0, bytes_accessed=8 << 20, transcendentals=0),
         name="join",
     )(*parts)
@@ -445,12 +442,15 @@
     other_main = swap_cores(main)
     a2, b1 = send(piece_a, ring("y", 2)), send(piece_b, ring("z", 1))
     tail = ring_z[part:]
-    main, other_main, tail, a2, b1, piece_b = tie(main, other_main, tail, a2, b1, piece_b)
+    main, other_main, tail = tie(main, other_main, tail)
     corners = [tail] + [send(tail, lambda X, Y, Z, C, d=d: (X - d, Y, Z, C)) for d in (1, 2, 3)]
-    b2, b3 = send(piece_b, ring("z", 2)), send(piece_b, ring("z", 3))
 
     place = (jnp.stack([x, core]),)
     state = squares(first_kernel, "open0", 4, 0, main, other_main, place=place)
+
+    state, a2, b1, piece_b = tie(state, a2, b1, piece_b)
+    b2, b3 = send(piece_b, ring("z", 2)), send(piece_b, ring("z", 3))
+    state = squares(middle_kernel, "middle0", 4, 0, *state)
 
     state, b2, b3, corners = tie(state, b2, b3, corners)
     corner = jnp.concatenate(corners, axis=0)

time: 389 us -> 271 us (0.70)
  Pallas kernels: 240 us -> 122 us
  local copies, waits for them, and re-layouts: 17.1 us -> 22.5 us
    pallas_call x1, Pallas kernels: 128 us -> 0.27 us  [join(): pl.pallas_call(join_kernel, out_shape=(jax.ShapeDtypeStruct((4 * TILE, ED...]
    unnamed x54 -> x64, local copies, waits for them, and re-layouts: 7.64 us -> 19.1 us
    pallas_call x4 -> x5, Pallas kernels: 72.2 us -> 81.8 us  [squares(): pl.pallas_call(kernel, out_shape=(jax.ShapeDtypeStruct((NB, NB), F32),) *...]
  transfers between devices with their start and end apart: 40 -> 40, of which waited for: 13 -> 17; matrix products, arithmetic and copies ran while one was open for 2% -> 2% of each run, Pallas kernels for 56% -> 36%
where the time goes in v4:
time: 271 us; the launch traced here: 266 us
  Pallas kernels  122 us (45%)
  starting transfers between devices  63.4 us (23%)
  waiting for transfers between devices  49 us (18%)
  local copies, waits for them, and re-layouts  22.5 us (8%)
  other arithmetic  7.25 us (3%)
    pallas_call x5, Pallas kernels, squares(): pl.pallas_call(kernel, out_shape=(jax.ShapeDtypeStruct((NB, NB), F32),) *...  81.8 us
    ppermute x40, starting transfers between devices, send(): return lax.ppermute(value, AXES, route(rule))  63.4 us
    ppermute x40, waiting for transfers between devices, send(): return lax.ppermute(value, AXES, route(rule))  49 us
    pallas_call x1, Pallas kernels, body(): pl.pallas_call(update_kernel, in_specs=[pl.BlockSpec(memory_space=pltpu.S...  27.7 us
    unnamed x64, local copies, waits for them, and re-layouts  19.1 us
    pallas_call x1, Pallas kernels, body(): pl.pallas_call(solve_kernel, out_shape=(jax.ShapeDtypeStruct((3 * EDGE, w...  12 us
  transfers between devices with their start and end apart: 40, of which 17 were waited for; matrix products, arithmetic and copies ran while one was open for 2% of the time, Pallas kernels for 36%

profile of v4, /device:TPU:1, one launch (start us, length us, event | category | flops | bytes accessed | tf_op | source)
XLA Modules:
  0.0 265.9 jit_solution(5113689217923221387)
XLA Ops:
  2.0 4.0 %collective-permute-start = (f32[128,512]{1,0:T(8,128)S(1)}, f32[128,512]{1,0:T(8,128)S(1)}, u32[]{:S(2)}, u32[]{:S(2)}) collective-permute-start(f32[128,512]{1,0:T(8,128)S(1)} %get-tuple-element.152), channel_id=1, source_target_pairs={{0,64},{32,96},{1,65},{33,97}} | collective-permute-start | bytes 786440 | tf_op jit(solution)/shard_map/ppermute | solution.py:37
  6.0 2.6 collective-permute-start.2
  8.6 3.1 %collective-permute-start.1 = (f32[128,512]{1,0:T(8,128)S(1)}, f32[128,512]{1,0:T(8,128)}, u32[]{:S(2)}, u32[]{:S(2)}) collective-permute-start(f32[128,512]{1,0:T(8,128)S(1)} %get-tuple-element.154), channel_id=1, source_target_pairs={{0,1},{32,33},{1,0},{33,32}} | collective-permute-start | bytes 786440 | tf_op jit(solution)/shard_map/ppermute | solution.py:37
  13.5 6.6 %collective-permute-done.1 = f32[128,512]{1,0:T(8,128)} collective-permute-done((f32[128,512]{1,0:T(8,128)S(1)}, f32[128,512]{1,0:T(8,128)}, u32[]{:S(2)}, u32[]{:S(2)}) %collective-permute-start.1) | collective-permute-done | bytes 262176 | tf_op jit(solution)/shard_map/ppermute | solution.py:37
  23.2 2.1 collective-permute-start.6
  30.9 2.3 collective-permute-done.4
  34.1 4.4 %collective-permute-done.7 = f32[256,512]{1,0:T(8,128)} collective-permute-done((f32[256,512]{1,0:T(8,128)S(1)}, f32[256,512]{1,0:T(8,128)}, u32[]{:S(2)}, u32[]{:S(2)}) %collective-permute-start.7) | collective-permute-done | bytes 524320 | tf_op jit(solution)/shard_map/ppermute | solution.py:37
  41.1 2.0 collective-permute-start.8
  44.5 4.3 %collective-permute-start.14 = (f32[256,512]{1,0:T(8,128)S(1)}, f32[256,512]{1,0:T(8,128)S(1)}, u32[]{:S(2)}, u32[]{:S(2)}) collective-permute-start(f32[256,512]{1,0:T(8,128)S(1)} %constant_dynamic-slice_fusion.1), channel_id=1, source_target_pairs={{0,2},{32,1},{8,10},{40,9},{16,18},{48,17},{24,26},{56,25},{2,64},... | collective-permute-start | bytes 1572872 | tf_op jit(solution)/shard_map/ppermute | solution.py:37
  51.2 3.8 %collective-permute-done.13 = f32[64,512]{1,0:T(8,128)S(1)} collective-permute-done((f32[64,512]{1,0:T(8,128)S(1)}, f32[64,512]{1,0:T(8,128)S(1)}, u32[]{:S(2)}, u32[]{:S(2)}) %collective-permute-start.13) | collective-permute-done | bytes 131104 | tf_op jit(solution)/shard_map/ppermute | solution.py:37
  55.7 2.0 collective-permute-done.11
  60.9 2.7 %collective-permute-start.19 = (f32[128,1024]{1,0:T(8,128)S(1)}, f32[128,1024]{1,0:T(8,128)S(1)}, u32[]{:S(2)}, u32[]{:S(2)}) collective-permute-start(f32[128,1024]{1,0:T(8,128)S(1)} %get-tuple-element.89.refs_0_), channel_id=1, source_target_pairs={{0,6},{32,38},{8,14},{40,46},{16,22},{48,54},{24,30},{56,62},{2,0}... | collective-permute-start | bytes 1572872 | tf_op jit(solution)/shard_map/ppermute | solution.py:37
  64.9 2.0 collective-permute-start.16
  66.8 11.4 %collective-permute-done.18 = f32[128,512]{1,0:T(8,128)S(1)} collective-permute-done((f32[128,512]{1,0:T(8,128)S(1)}, f32[128,512]{1,0:T(8,128)S(1)}, u32[]{:S(2)}, u32[]{:S(2)}) %collective-permute-start.18) | collective-permute-done | bytes 262176 | tf_op jit(solution)/shard_map/ppermute | solution.py:37
  81.7 2.1 collective-permute-done.21.other
  84.3 3.1 %collective-permute-start.27 = (f32[128,512]{1,0:T(8,128)S(1)}, f32[128,512]{1,0:T(8,128)S(1)}, u32[]{:S(2)}, u32[]{:S(2)}) collective-permute-start(f32[128,512]{1,0:T(8,128)S(1)} %get-tuple-element.101), channel_id=1, source_target_pairs={{0,1},{32,33},{8,9},{40,41},{16,17},{48,49},{24,25},{56,57},{2,3},... | collective-permute-start | bytes 786440 | tf_op jit(solution)/shard_map/ppermute | solution.py:37
  87.4 9.2 %open0.1 = (f32[512,512]{1,0:T(8,128)S(1)}, f32[512,512]{1,0:T(8,128)S(1)}, f32[512,512]{1,0:T(8,128)S(1)}, f32[512,512]{1,0:T(8,128)S(1)}) custom-call(s32[2]{0:T(128)S(1)} %pad_add_fusion.1.place, f32[512,512]{1,0:T(8,128)S(1)} %pad_maximum_fusion.mine, f32[512,512]{1,0:T(8,128)S(1)} %collective-permute-done.21.other), custom_call_target="tpu_custom_call" | custom-call | flops 30000001024 | bytes 2097152 | tf_op jit(solution)/shard_map/open0/pallas_call | solution.py:215
  100.0 8.2 %middle0.1 = (f32[512,512]{1,0:T(8,128)S(1)}, f32[512,512]{1,0:T(8,128)S(1)}, f32[512,512]{1,0:T(8,128)S(1)}, f32[512,512]{1,0:T(8,128)S(1)}) custom-call(f32[512,512]{1,0:T(8,128)S(1)} %get-tuple-element.91.m, f32[512,512]{1,0:T(8,128)S(1)} %get-tuple-element.92.l, f32[512,512]{1,0:T(8,128)S(1)} %get-tuple-element.93.i, f32[512,512]{1,0:T(8,128)S(1)} %get-tuple-element.94.t), custom_call_target="tpu_custom_call" | custom-call | flops 30000001024 | bytes 4194304 | tf_op jit(solution)/shard_map/middle0/pallas_call | solution.py:215
  114.5 7.3 %collective-permute-done.24.refs_6_ = f32[128,1024]{1,0:T(8,128)S(1)} collective-permute-done((f32[128,1024]{1,0:T(8,128)S(1)}, f32[128,1024]{1,0:T(8,128)S(1)}, u32[]{:S(2)}, u32[]{:S(2)}) %collective-permute-start.24) | collective-permute-done | bytes 524320 | tf_op jit(solution)/shard_map/ppermute | solution.py:37
  125.5 4.1 %collective-permute-start.29 = (f32[512,512]{1,0:T(8,128)}, f32[512,512]{1,0:T(8,128)}, u32[]{:S(2)}, u32[]{:S(2)}) collective-permute-start(f32[512,512]{1,0:T(8,128)} %constant_dynamic-update-slice_fusion.edge), channel_id=1, source_target_pairs={{0,32},{32,0},{8,40},{40,8},{16,48},{48,16},{24,56},{56,24},{2,34}... | collective-permute-start | bytes 3145736 | tf_op jit(solution)/shard_map/ppermute | solution.py:37
  136.3 2.7 %collective-permute-start.30 = (f32[512,1024]{1,0:T(8,128)S(1)}, f32[512,1024]{1,0:T(8,128)S(1)}, u32[]{:S(2)}, u32[]{:S(2)}) collective-permute-start(f32[512,1024]{1,0:T(8,128)S(1)} %get-tuple-element.123.refs_0_), channel_id=1, source_target_pairs={{0,24},{32,56},{8,0},{40,32},{16,8},{48,40},{24,16},{56,48},{2,26}... | collective-permute-start | bytes 6291464 | tf_op jit(solution)/shard_map/ppermute | solution.py:37
  139.0 2.7 %collective-permute-start.32 = (f32[512,1024]{1,0:T(8,128)S(1)}, f32[512,1024]{1,0:T(8,128)S(1)}, u32[]{:S(2)}, u32[]{:S(2)}) collective-permute-start(f32[512,1024]{1,0:T(8,128)S(1)} %get-tuple-element.124.refs_5_), channel_id=1, source_target_pairs={{0,6},{32,38},{8,14},{40,46},{16,22},{48,54},{24,30},{56,62},{2,0}... | collective-permute-start | bytes 6291464 | tf_op jit(solution)/shard_map/ppermute | solution.py:37
  141.8 3.4 %collective-permute-start.34 = (f32[512,768]{1,0:T(8,128)S(1)}, f32[512,768]{1,0:T(8,128)S(1)}, u32[]{:S(2)}, u32[]{:S(2)}) collective-permute-start(f32[512,768]{1,0:T(8,128)S(1)} %constant_dynamic-update-slice_fusion.4), channel_id=1, source_target_pairs={{0,64},{32,96},{8,72},{40,104},{16,80},{48,112},{24,88},{56,120},{... | collective-permute-start | bytes 4718600 | tf_op jit(solution)/shard_map/ppermute | solution.py:37
  145.2 21.8 %below0.1 = (f32[512,512]{1,0:T(8,128)S(1)}, f32[512,512]{1,0:T(8,128)S(1)}, f32[512,512]{1,0:T(8,128)S(1)}, f32[512,512]{1,0:T(8,128)S(1)}, f32[512,512]{1,0:T(8,128)S(1)}, /*index=5*/f32[512,512]{1,0:T(8,128)S(1)}) custom-call(s32[2]{0:T(128)S(1)} %pad_add_fusion.1.place, f32[512,512]{1,0:T(8,128)S(1)} %copy-done.19, f32[512,512]{1,0:T(8,128)S(1)} %copy-done.21, ...), custom_call_target="tpu_custom_call" | custom-call | flops 30000001024 | bytes 8388608 | tf_op jit(solution)/shard_map/below0/pallas_call | solution.py:215
  167.1 16.4 %open1.1 = (f32[512,512]{1,0:T(8,128)S(1)}, f32[512,512]{1,0:T(8,128)S(1)}, f32[512,512]{1,0:T(8,128)S(1)}, f32[512,512]{1,0:T(8,128)S(1)}) custom-call(f32[512,512]{1,0:T(8,128)S(1)} %get-tuple-element.112.source), custom_call_target="tpu_custom_call" | custom-call | flops 30000001024 | bytes 1048576 | tf_op jit(solution)/shard_map/open1/pallas_call | solution.py:215
  184.8 2.0 collective-permute-done.33.refs_7_
  188.3 2.7 %collective-permute-start.38 = (f32[256,1024]{1,0:T(8,128)S(1)}, f32[256,1024]{1,0:T(8,128)S(1)}, u32[]{:S(2)}, u32[]{:S(2)}) collective-permute-start(f32[256,1024]{1,0:T(8,128)S(1)} %slice.57), channel_id=1, source_target_pairs={{0,6},{32,38},{8,14},{40,46},{16,22},{48,54},{24,30},{56,62},{2,0}... | collective-permute-start | bytes 3145736 | tf_op jit(solution)/shard_map/ppermute | solution.py:37
  191.0 2.7 %collective-permute-start.36 = (f32[256,1024]{1,0:T(8,128)S(1)}, f32[256,1024]{1,0:T(8,128)S(1)}, u32[]{:S(2)}, u32[]{:S(2)}) collective-permute-start(f32[256,1024]{1,0:T(8,128)S(1)} %slice.55), channel_id=1, source_target_pairs={{0,24},{32,56},{8,0},{40,32},{16,8},{48,40},{24,16},{56,48},{2,26}... | collective-permute-start | bytes 3145736 | tf_op jit(solution)/shard_map/ppermute | solution.py:37
  193.9 2.6 collective-permute-start.35
  196.5 26.2 %close1.1 = (f32[512,512]{1,0:T(8,128)S(1)}, f32[512,512]{1,0:T(8,128)S(1)}, f32[512,512]{1,0:T(8,128)S(1)}) custom-call(f32[512,512]{1,0:T(8,128)S(1)} %get-tuple-element.130.m, f32[512,512]{1,0:T(8,128)S(1)} %get-tuple-element.131.l, f32[512,512]{1,0:T(8,128)S(1)} %get-tuple-element.132.i, f32[512,512]{1,0:T(8,128)S(1)} %get-tuple-element.133.t), custom_call_target="tpu_custom_call" | custom-call | flops 30000001024 | bytes 4194304 | tf_op jit(solution)/shard_map/close1/pallas_call | solution.py:215
  225.9 12.0 %solve.1 = (bf16[3072,768]{1,0:T(8,128)(2,1)}, f32[1024,256]{1,0:T(8,128)S(1)}) custom-call(s32[1]{0:T(128)} %bitcast.1.col_ref, f32[512,768]{1,0:T(8,128)} %get-tuple-element.145.g0, f32[512,768]{1,0:T(8,128)} %get-tuple-element.144.g1, f32[512,512]{1,0:T(8,128)S(1)} %get-tuple-element.126.inv0, f32[512,512]{1,0:T(8,128)S(1)} %get-tuple-element.127.inv0_t, ...), custom_call_target="tpu_custom_call" | custom-call | flops 10000000000 | bytes 16777216 | tf_op jit(solution)/shard_map/solve/pallas_call | solution.py:485
  238.0 27.7 %update.1 = (f32[4096,512]{1,0:T(8,128)}, f32[4096,256]{1,0:T(8,128)}) custom-call(s32[4]{0:T(128)S(1)} %pad_add_fusion.place, bf16[3072,768]{1,0:T(8,128)(2,1)} %get-tuple-element.136.weights, f32[512,512]{1,0:T(8,128)S(1)} %select_select_fusion.special, f32[512,256]{1,0:T(8,128)S(1)} %constant_dynamic-slice_fusion.y, f32[512,1024]{1,0:T(8,128)} %copy-done.12, ...), custom_call_target="tpu_custom_call" | custom-call | flops 20000000000 | bytes 46137344 | tf_op jit(solution)/shard_map/update/pallas_call | solution.py:505
  (150 shorter events, 54.3 us)
Async XLA Ops:
  2.0 10.1 %collective-permute-start = (f32[128,512]{1,0:T(8,128)S(1)}, f32[128,512]{1,0:T(8,128)S(1)}, u32[]{:S(2)}, u32[]{:S(2)}) collective-permute-start(f32[128,512]{1,0:T(8,128)S(1)} %get-tuple-element.152), channel_id=1, source_target_pairs={{0,64},{32,96},{1,65},{33,97}} | collective-permute-start | bytes 786440 | tf_op jit(solution)/shard_map/ppermute | solution.py:37
  8.6 11.6 %collective-permute-start.1 = (f32[128,512]{1,0:T(8,128)S(1)}, f32[128,512]{1,0:T(8,128)}, u32[]{:S(2)}, u32[]{:S(2)}) collective-permute-start(f32[128,512]{1,0:T(8,128)S(1)} %get-tuple-element.154), channel_id=1, source_target_pairs={{0,1},{32,33},{1,0},{33,32}} | collective-permute-start | bytes 786440 | tf_op jit(solution)/shard_map/ppermute | solution.py:37
  21.3 17.2 %collective-permute-start.7 = (f32[256,512]{1,0:T(8,128)S(1)}, f32[256,512]{1,0:T(8,128)}, u32[]{:S(2)}, u32[]{:S(2)}) collective-permute-start(f32[256,512]{1,0:T(8,128)S(1)} %constant_dynamic-slice_fusion.2), channel_id=1, source_target_pairs={{0,1},{32,2},{8,9},{40,10},{16,17},{48,18},{24,25},{56,26},{2,67},... | collective-permute-start | bytes 1572872 | tf_op jit(solution)/shard_map/ppermute | solution.py:37
  23.2 15.3 %collective-permute-start.6 = (f32[256,512]{1,0:T(8,128)S(1)}, f32[256,512]{1,0:T(8,128)}, u32[]{:S(2)}, u32[]{:S(2)}) collective-permute-start(f32[256,512]{1,0:T(8,128)S(1)} %constant_dynamic-slice_fusion.2), channel_id=1, source_target_pairs={{0,0},{32,3},{8,8},{40,11},{16,16},{48,19},{24,24},{56,27},{2,66},... | collective-permute-start | bytes 1572872 | tf_op jit(solution)/shard_map/ppermute | solution.py:37
  38.5 10.2 %collective-permute-start.10 = (f32[64,512]{1,0:T(8,128)S(1)}, f32[64,512]{1,0:T(8,128)S(1)}, u32[]{:S(2)}, u32[]{:S(2)}) collective-permute-start(f32[64,512]{1,0:T(8,128)S(1)} %add_add_fusion.1), channel_id=1, source_target_pairs={{0,6},{32,38},{8,14},{40,46},{16,22},{48,54},{24,30},{56,62},{64,7... | collective-permute-start | bytes 393224 | tf_op jit(solution)/shard_map/ppermute | solution.py:37
  39.8 9.0 %collective-permute-start.9 = (f32[64,512]{1,0:T(8,128)S(1)}, f32[64,512]{1,0:T(8,128)S(1)}, u32[]{:S(2)}, u32[]{:S(2)}) collective-permute-start(f32[64,512]{1,0:T(8,128)S(1)} %add_add_fusion.1), channel_id=1, source_target_pairs={{0,4},{32,36},{8,12},{40,44},{16,20},{48,52},{24,28},{56,60},{64,6... | collective-permute-start | bytes 393224 | tf_op jit(solution)/shard_map/ppermute | solution.py:37
  43.1 14.7 %collective-permute-start.15 = (f32[256,512]{1,0:T(8,128)S(1)}, f32[256,512]{1,0:T(8,128)S(1)}, u32[]{:S(2)}, u32[]{:S(2)}) collective-permute-start(f32[256,512]{1,0:T(8,128)S(1)} %constant_dynamic-slice_fusion.1), channel_id=1, source_target_pairs={{0,3},{32,0},{8,11},{40,8},{16,19},{48,16},{24,27},{56,24},{2,65},... | collective-permute-start | bytes 1572872 | tf_op jit(solution)/shard_map/ppermute | solution.py:37
  44.5 14.8 %collective-permute-start.14 = (f32[256,512]{1,0:T(8,128)S(1)}, f32[256,512]{1,0:T(8,128)S(1)}, u32[]{:S(2)}, u32[]{:S(2)}) collective-permute-start(f32[256,512]{1,0:T(8,128)S(1)} %constant_dynamic-slice_fusion.1), channel_id=1, source_target_pairs={{0,2},{32,1},{8,10},{40,9},{16,18},{48,17},{24,26},{56,25},{2,64},... | collective-permute-start | bytes 1572872 | tf_op jit(solution)/shard_map/ppermute | solution.py:37
  49.9 7.9 %collective-permute-start.11 = (f32[64,512]{1,0:T(8,128)S(1)}, f32[64,512]{1,0:T(8,128)S(1)}, u32[]{:S(2)}, u32[]{:S(2)}) collective-permute-start(f32[64,512]{1,0:T(8,128)S(1)} %add_add_fusion), channel_id=1, source_target_pairs={{0,8},{32,40},{8,16},{40,48},{16,24},{48,56},{24,0},{56,32},{2,10}... | collective-permute-start | bytes 393224 | tf_op jit(solution)/shard_map/ppermute | solution.py:37
  60.8 17.8 %collective-permute-start.20 = (f32[128,1024]{1,0:T(8,128)S(1)}, f32[128,1024]{1,0:T(8,128)S(1)}, u32[]{:S(2)}, u32[]{:S(2)}) collective-permute-start(f32[128,1024]{1,0:T(8,128)S(1)} %get-tuple-element.89.refs_0_), channel_id=1, source_target_pairs={{0,2},{32,34},{8,10},{40,42},{16,18},{48,50},{24,26},{56,58},{2,4}... | collective-permute-start | bytes 1572872 | tf_op jit(solution)/shard_map/ppermute | solution.py:37
  60.9 18.6 %collective-permute-start.19 = (f32[128,1024]{1,0:T(8,128)S(1)}, f32[128,1024]{1,0:T(8,128)S(1)}, u32[]{:S(2)}, u32[]{:S(2)}) collective-permute-start(f32[128,1024]{1,0:T(8,128)S(1)} %get-tuple-element.89.refs_0_), channel_id=1, source_target_pairs={{0,6},{32,38},{8,14},{40,46},{16,22},{48,54},{24,30},{56,62},{2,0}... | collective-permute-start | bytes 1572872 | tf_op jit(solution)/shard_map/ppermute | solution.py:37
  63.6 14.7 %collective-permute-start.18 = (f32[128,512]{1,0:T(8,128)S(1)}, f32[128,512]{1,0:T(8,128)S(1)}, u32[]{:S(2)}, u32[]{:S(2)}) collective-permute-start(f32[128,512]{1,0:T(8,128)S(1)} %get-tuple-element.156), channel_id=1, source_target_pairs={{0,64},{32,96},{8,72},{40,104},{16,80},{48,112},{24,88},{56,120},{... | collective-permute-start | bytes 786440 | tf_op jit(solution)/shard_map/ppermute | solution.py:37
  63.7 14.6 %collective-permute-start.17 = (f32[128,512]{1,0:T(8,128)S(1)}, f32[128,512]{1,0:T(8,128)S(1)}, u32[]{:S(2)}, u32[]{:S(2)}) collective-permute-start(f32[128,512]{1,0:T(8,128)S(1)} %get-tuple-element.156), channel_id=1, source_target_pairs={{0,1},{32,33},{8,9},{40,41},{16,17},{48,49},{24,25},{56,57},{2,3},... | collective-permute-start | bytes 786440 | tf_op jit(solution)/shard_map/ppermute | solution.py:37
  64.9 13.7 %collective-permute-start.16 = (f32[128,512]{1,0:T(8,128)S(1)}, f32[128,512]{1,0:T(8,128)S(1)}, u32[]{:S(2)}, u32[]{:S(2)}) collective-permute-start(f32[128,512]{1,0:T(8,128)S(1)} %get-tuple-element.156), channel_id=1, source_target_pairs={{0,65},{32,97},{8,73},{40,105},{16,81},{48,113},{24,89},{56,121},{... | collective-permute-start | bytes 786440 | tf_op jit(solution)/shard_map/ppermute | solution.py:37
  81.6 15.1 %collective-permute-start.22 = (f32[128,1024]{1,0:T(8,128)S(1)}, f32[128,1024]{1,0:T(8,128)S(1)}, u32[]{:S(2)}, u32[]{:S(2)}) collective-permute-start(f32[128,1024]{1,0:T(8,128)S(1)} %get-tuple-element.89.refs_0_), channel_id=1, source_target_pairs={{0,4},{32,36},{8,12},{40,44},{16,20},{48,52},{24,28},{56,60},{2,6}... | collective-permute-start | bytes 1572872 | tf_op jit(solution)/shard_map/ppermute | solution.py:37
  81.6 15.8 %collective-permute-start.23 = (f32[128,1024]{1,0:T(8,128)S(1)}, f32[128,1024]{1,0:T(8,128)S(1)}, u32[]{:S(2)}, u32[]{:S(2)}) collective-permute-start(f32[128,1024]{1,0:T(8,128)S(1)} %get-tuple-element.99.refs_4_), channel_id=1, source_target_pairs={{0,24},{32,56},{8,0},{40,32},{16,8},{48,40},{24,16},{56,48},{2,26}... | collective-permute-start | bytes 1572872 | tf_op jit(solution)/shard_map/ppermute | solution.py:37
  83.8 28.3 %collective-permute-start.28 = (f32[128,512]{1,0:T(8,128)S(1)}, f32[128,512]{1,0:T(8,128)S(1)}, u32[]{:S(2)}, u32[]{:S(2)}) collective-permute-start(f32[128,512]{1,0:T(8,128)S(1)} %get-tuple-element.101), channel_id=1, source_target_pairs={{0,64},{32,96},{8,72},{40,104},{16,80},{48,112},{24,88},{56,120},{... | collective-permute-start | bytes 786440 | tf_op jit(solution)/shard_map/ppermute | solution.py:37
  84.3 27.9 %collective-permute-start.27 = (f32[128,512]{1,0:T(8,128)S(1)}, f32[128,512]{1,0:T(8,128)S(1)}, u32[]{:S(2)}, u32[]{:S(2)}) collective-permute-start(f32[128,512]{1,0:T(8,128)S(1)} %get-tuple-element.101), channel_id=1, source_target_pairs={{0,1},{32,33},{8,9},{40,41},{16,17},{48,49},{24,25},{56,57},{2,3},... | collective-permute-start | bytes 786440 | tf_op jit(solution)/shard_map/ppermute | solution.py:37
  87.4 24.8 %collective-permute-start.26 = (f32[128,512]{1,0:T(8,128)S(1)}, f32[128,512]{1,0:T(8,128)S(1)}, u32[]{:S(2)}, u32[]{:S(2)}) collective-permute-start(f32[128,512]{1,0:T(8,128)S(1)} %get-tuple-element.101), channel_id=1, source_target_pairs={{0,65},{32,97},{8,73},{40,105},{16,81},{48,113},{24,89},{56,121},{... | collective-permute-start | bytes 786440 | tf_op jit(solution)/shard_map/ppermute | solution.py:37
  98.3 15.4 %collective-permute-start.25 = (f32[128,1024]{1,0:T(8,128)S(1)}, f32[128,1024]{1,0:T(8,128)S(1)}, u32[]{:S(2)}, u32[]{:S(2)}) collective-permute-start(f32[128,1024]{1,0:T(8,128)S(1)} %get-tuple-element.99.refs_4_), channel_id=1, source_target_pairs={{0,8},{32,40},{8,16},{40,48},{16,24},{48,56},{24,0},{56,32},{2,10}... | collective-permute-start | bytes 1572872 | tf_op jit(solution)/shard_map/ppermute | solution.py:37
  98.3 23.5 %collective-permute-start.24 = (f32[128,1024]{1,0:T(8,128)S(1)}, f32[128,1024]{1,0:T(8,128)S(1)}, u32[]{:S(2)}, u32[]{:S(2)}) collective-permute-start(f32[128,1024]{1,0:T(8,128)S(1)} %get-tuple-element.99.refs_4_), channel_id=1, source_target_pairs={{0,16},{32,48},{8,24},{40,56},{16,0},{48,32},{24,8},{56,40},{2,18}... | collective-permute-start | bytes 1572872 | tf_op jit(solution)/shard_map/ppermute | solution.py:37
  125.5 16.2 %collective-permute-start.29 = (f32[512,512]{1,0:T(8,128)}, f32[512,512]{1,0:T(8,128)}, u32[]{:S(2)}, u32[]{:S(2)}) collective-permute-start(f32[512,512]{1,0:T(8,128)} %constant_dynamic-update-slice_fusion.edge), channel_id=1, source_target_pairs={{0,32},{32,0},{8,40},{40,8},{16,48},{48,16},{24,56},{56,24},{2,34}... | collective-permute-start | bytes 3145736 | tf_op jit(solution)/shard_map/ppermute | solution.py:37
  136.2 48.5 %collective-permute-start.31 = (f32[512,1024]{1,0:T(8,128)S(1)}, f32[512,1024]{1,0:T(8,128)S(1)}, u32[]{:S(2)}, u32[]{:S(2)}) collective-permute-start(f32[512,1024]{1,0:T(8,128)S(1)} %get-tuple-element.123.refs_0_), channel_id=1, source_target_pairs={{0,8},{32,40},{8,16},{40,48},{16,24},{48,56},{24,0},{56,32},{2,10}... | collective-permute-start | bytes 6291464 | tf_op jit(solution)/shard_map/ppermute | solution.py:37
  136.3 48.5 %collective-permute-start.30 = (f32[512,1024]{1,0:T(8,128)S(1)}, f32[512,1024]{1,0:T(8,128)S(1)}, u32[]{:S(2)}, u32[]{:S(2)}) collective-permute-start(f32[512,1024]{1,0:T(8,128)S(1)} %get-tuple-element.123.refs_0_), channel_id=1, source_target_pairs={{0,24},{32,56},{8,0},{40,32},{16,8},{48,40},{24,16},{56,48},{2,26}... | collective-permute-start | bytes 6291464 | tf_op jit(solution)/shard_map/ppermute | solution.py:37
  139.0 47.8 %collective-permute-start.33 = (f32[512,1024]{1,0:T(8,128)S(1)}, f32[512,1024]{1,0:T(8,128)S(1)}, u32[]{:S(2)}, u32[]{:S(2)}) collective-permute-start(f32[512,1024]{1,0:T(8,128)S(1)} %get-tuple-element.124.refs_5_), channel_id=1, source_target_pairs={{0,2},{32,34},{8,10},{40,42},{16,18},{48,50},{24,26},{56,58},{2,4}... | collective-permute-start | bytes 6291464 | tf_op jit(solution)/shard_map/ppermute | solution.py:37
  139.0 47.8 %collective-permute-start.32 = (f32[512,1024]{1,0:T(8,128)S(1)}, f32[512,1024]{1,0:T(8,128)S(1)}, u32[]{:S(2)}, u32[]{:S(2)}) collective-permute-start(f32[512,1024]{1,0:T(8,128)S(1)} %get-tuple-element.124.refs_5_), channel_id=1, source_target_pairs={{0,6},{32,38},{8,14},{40,46},{16,22},{48,54},{24,30},{56,62},{2,0}... | collective-permute-start | bytes 6291464 | tf_op jit(solution)/shard_map/ppermute | solution.py:37
  141.8 45.0 %collective-permute-start.34 = (f32[512,768]{1,0:T(8,128)S(1)}, f32[512,768]{1,0:T(8,128)S(1)}, u32[]{:S(2)}, u32[]{:S(2)}) collective-permute-start(f32[512,768]{1,0:T(8,128)S(1)} %constant_dynamic-update-slice_fusion.4), channel_id=1, source_target_pairs={{0,64},{32,96},{8,72},{40,104},{16,80},{48,112},{24,88},{56,120},{... | collective-permute-start | bytes 4718600 | tf_op jit(solution)/shard_map/ppermute | solution.py:37
  188.2 49.7 %collective-permute-start.39 = (f32[256,1024]{1,0:T(8,128)S(1)}, f32[256,1024]{1,0:T(8,128)S(1)}, u32[]{:S(2)}, u32[]{:S(2)}) collective-permute-start(f32[256,1024]{1,0:T(8,128)S(1)} %slice.58), channel_id=1, source_target_pairs={{0,2},{32,34},{8,10},{40,42},{16,18},{48,50},{24,26},{56,58},{2,4}... | collective-permute-start | bytes 3145736 | tf_op jit(solution)/shard_map/ppermute | solution.py:37
  188.3 49.6 %collective-permute-start.38 = (f32[256,1024]{1,0:T(8,128)S(1)}, f32[256,1024]{1,0:T(8,128)S(1)}, u32[]{:S(2)}, u32[]{:S(2)}) collective-permute-start(f32[256,1024]{1,0:T(8,128)S(1)} %slice.57), channel_id=1, source_target_pairs={{0,6},{32,38},{8,14},{40,46},{16,22},{48,54},{24,30},{56,62},{2,0}... | collective-permute-start | bytes 3145736 | tf_op jit(solution)/shard_map/ppermute | solution.py:37
  191.0 47.0 %collective-permute-start.37 = (f32[256,1024]{1,0:T(8,128)S(1)}, f32[256,1024]{1,0:T(8,128)S(1)}, u32[]{:S(2)}, u32[]{:S(2)}) collective-permute-start(f32[256,1024]{1,0:T(8,128)S(1)} %slice.56), channel_id=1, source_target_pairs={{0,8},{32,40},{8,16},{40,48},{16,24},{48,56},{24,0},{56,32},{2,10}... | collective-permute-start | bytes 3145736 | tf_op jit(solution)/shard_map/ppermute | solution.py:37
  191.0 47.0 %collective-permute-start.36 = (f32[256,1024]{1,0:T(8,128)S(1)}, f32[256,1024]{1,0:T(8,128)S(1)}, u32[]{:S(2)}, u32[]{:S(2)}) collective-permute-start(f32[256,1024]{1,0:T(8,128)S(1)} %slice.55), channel_id=1, source_target_pairs={{0,24},{32,56},{8,0},{40,32},{16,8},{48,40},{24,16},{56,48},{2,26}... | collective-permute-start | bytes 3145736 | tf_op jit(solution)/shard_map/ppermute | solution.py:37
  193.9 30.1 %collective-permute-start.35 = (f32[512,768]{1,0:T(8,128)S(1)}, f32[512,768]{1,0:T(8,128)S(1)}, u32[]{:S(2)}, u32[]{:S(2)}) collective-permute-start(f32[512,768]{1,0:T(8,128)S(1)} %broadcast_select_fusion), channel_id=1, source_target_pairs={{0,32},{32,0},{8,40},{40,8},{16,48},{48,16},{24,56},{56,24},{2,34}... | collective-permute-start | bytes 4718600 | tf_op jit(solution)/shard_map/ppermute | solution.py:37
  (39 other events, 165.1 us)
